TPU v7x, 256 devices: a whole 4x4x8 slice. The times are simulated.
256 devices in a mesh: ctx: 64 (over z, y, core), kvh: 4 (over x).
Axes of the slice: x: 4, y: 4, z: 8, core: 2. Of those that a mesh axis runs over, the one named last changes fastest.
Arguments:
- tokens: bfloat16 [32768, 4096], P('ctx', 'kvh'), may hold values from -6 to 6
- norm_gain: float32 [4096], replicated, may hold values from 0.1 to 1.9
- w_query: bfloat16 [4096, 2048], P(None, 'kvh'), may hold values from -0.09375 to 0.09375
- w_key: bfloat16 [4096, 512], P(None, 'kvh'), may hold values from -0.09375 to 0.09375
- w_value: bfloat16 [4096, 512], P(None, 'kvh'), may hold values from -0.09375 to 0.09375
- w_out: bfloat16 [2048, 4096], P('kvh'), may hold values from -0.125 to 0.125
- picks: int32 [64, 4, 3], P('ctx', 'kvh'), may hold values from 0 to 62, as said below
Outputs:
- combined: bfloat16 [32768, 4096], P(('ctx', 'kvh'))
Inputs may be any that keep to these rules, and one draw needn't show every extreme that they name: `picks`: for block b > 0 and each KV head the 3 entries, where below b, are distinct, the first being b - 1; for b < 3 the entries that find no earlier block equal b and choose nothing.
All inputs are finite; a program needn't handle non-finite values.
Results may differ from a plain program's by a relative error of at most 0.018.
Values may be sent and summed in bfloat16 or wider, within the bound.
No kernel may reach another device: no remote copies, remote signals or barrier semaphores. Data moves between devices by JAX's collectives and lax.ppermute only.
A program may use at most 128 MiB of HBM per device.

v0:
```python
import jax
import jax.numpy as jnp
from jax import lax
from jax.experimental import pallas as pl
from jax.experimental.pallas import tpu as pltpu
from jax.sharding import PartitionSpec as P

HD = 128


ROPE_BASE = 500000.0


def turns(positions):
    half_dim = HD // 2
    frequency = ROPE_BASE ** (-jnp.arange(half_dim, dtype=jnp.float32) * 2.0 / HD)
    angles = positions.astype(jnp.float32)[:, None] * frequency[None, :]
    return jnp.cos(angles), jnp.sin(angles)


def rotate_pairs(head_rows, cosine, sine):
    cosine, sine = cosine[:, None, :], sine[:, None, :]
    lower_half = head_rows[..., : HD // 2]
    upper_half = head_rows[..., HD // 2 :]
    return jnp.concatenate(
        [lower_half * cosine - upper_half * sine, upper_half * cosine + lower_half * sine],
        axis=-1,
    )


SCALE = 1.4426950408889634 * HD**-0.5
MASKED = -1e30


def stack_heads(rows):
    return jnp.concatenate(
        [rows[:, h * HD : (h + 1) * HD] for h in range(rows.shape[1] // HD)], axis=0
    )


def scores_of(queries, keys):
    return lax.dot_general(
        queries, keys, (((1,), (1,)), ((), ())), preferred_element_type=jnp.float32
    )


def weigh(scores, offset, values):
    weights = jnp.exp2(scores * SCALE - offset).astype(jnp.bfloat16)
    wide = jnp.concatenate([values, jnp.ones_like(values)], axis=1)
    return jnp.dot(weights, wide, preferred_element_type=jnp.float32)


def row_max(scores):
    return jnp.max(scores, axis=1, keepdims=True)


def near_kernel(flag_ref, query_ref, own_ref, before_ref, sums_ref, stats_ref):
    block_len = query_ref.shape[0]
    quarter = block_len // RING
    heads = query_ref.shape[1] // HD
    stacked = quarter * heads
    has_before = flag_ref[0] > 0
    hidden = jnp.where(has_before, 0.0, -MASKED)
    row = lax.broadcasted_iota(jnp.int32, (stacked, quarter), 0) % quarter
    causal = lax.broadcasted_iota(jnp.int32, (stacked, quarter), 1) <= row
    left = lax.broadcasted_iota(jnp.int32, (stacked, HD), 1) < HD // 2
    for c in range(RING):
        start, end = c * quarter, (c + 1) * quarter
        queries = stack_heads(query_ref[start:end, :])
        own_scores = jnp.where(causal, scores_of(queries, own_ref[start:end, :]), MASKED)
        before_scores = scores_of(queries, before_ref[:block_len, :])
        top = jnp.maximum(
            row_max(own_scores), jnp.where(has_before, row_max(before_scores), MASKED)
        )
        if c:
            early_scores = scores_of(queries, own_ref[:start, :])
            top = jnp.maximum(top, row_max(early_scores))
        offset = top * SCALE
        sums = weigh(own_scores, offset, own_ref[block_len + start : block_len + end, :])
        sums += weigh(before_scores, offset + hidden, before_ref[block_len:, :])
        if c:
            sums += weigh(early_scores, offset, own_ref[block_len : block_len + start, :])
        rows = slice(c * stacked, (c + 1) * stacked)
        sums_ref[rows, :] = sums[:, :HD]
        stats_ref[rows, :] = jnp.where(left, sums[:, HD:], top)


def far_kernel(flag_ref, query_ref, got_ref, sums_ref, stats_ref, out_ref):
    block_len, width = query_ref.shape
    quarter = block_len // RING
    heads = width // HD
    stacked = quarter * heads
    pieces = got_ref.shape[0] // 2
    for c in range(RING):
        rows = slice(c * stacked, (c + 1) * stacked)
        queries = stack_heads(query_ref[c * quarter : (c + 1) * quarter, :])
        before_top = stats_ref[rows, HD // 2 : HD // 2 + 1]
        top, parts = before_top, []
        for r in range(2):
            scores = scores_of(queries, got_ref[:pieces, r].reshape(-1, HD))
            top = jnp.maximum(top, jnp.where(flag_ref[r + 1] > 0, row_max(scores), MASKED))
            parts.append(scores)
        offset = top * SCALE
        shrink = jnp.exp2((before_top - top) * SCALE)
        total = stats_ref[rows, :1] * shrink
        sums = sums_ref[rows, :] * shrink
        for r in range(2):
            hidden = jnp.where(flag_ref[r + 1] > 0, 0.0, -MASKED)
            more = weigh(parts[r], offset + hidden, got_ref[pieces:, r].reshape(-1, HD))
            sums += more[:, :HD]
            total += more[:, HD:]
        done = (sums / total).astype(jnp.bfloat16)
        for h in range(heads):
            out_ref[c * quarter : (c + 1) * quarter, h * HD : (h + 1) * HD] = done[
                h * quarter : (h + 1) * quarter
            ]


def route_kernel(wanted_ref, held_ref, out_ref):
    for i in range(out_ref.shape[0]):
        out_ref[i] = held_ref[wanted_ref[i]]


VMEM = pl.BlockSpec(memory_space=pltpu.VMEM)
SMEM = pl.BlockSpec(memory_space=pltpu.SMEM)


def call(kernel, out_shape, operands, flops, name):
    return pl.pallas_call(
        kernel,
        out_shape=out_shape,
        in_specs=[SMEM] + [VMEM] * (len(operands) - 1),
        out_specs=[VMEM] * len(out_shape),
        compiler_params=pltpu.CompilerParams(vmem_limit_bytes=40 * 2**20),
        cost_estimate=pl.CostEstimate(flops=flops, bytes_accessed=2**22, transcendentals=2**21),
        name=name,
    )(*operands)


def attend_near(flags, queries, own, before):
    block_len, width = queries.shape
    stacked = block_len * width // HD
    shape = jax.ShapeDtypeStruct((stacked, HD), jnp.float32)
    flops = 8 * stacked * block_len * HD
    return call(near_kernel, [shape, shape], (flags, queries, own, before), flops, "attend_near")


def attend_far(flags, queries, got, sums, stats):
    block_len, width = queries.shape
    shape = jax.ShapeDtypeStruct((block_len, width), jnp.bfloat16)
    flops = 8 * block_len * width * block_len
    return call(far_kernel, [shape], (flags, queries, got, sums, stats), flops, "attend_far")[0]


def route(wanted, held):
    shape = jax.ShapeDtypeStruct(wanted.shape + held.shape[1:], held.dtype)
    return call(route_kernel, [shape], (wanted, held), 2**20, "route")[0]


RING = 4
RIGHT = [(i, (i + 1) % RING) for i in range(RING)]
LEFT = [(i, (i - 1) % RING) for i in range(RING)]
EVEN = [(i, i ^ 1) for i in range(RING)]
ODD = [(i, RING - 1 - i) for i in range(RING)]


def project_out(attended, w_out, w_near, me):
    rows, depth = attended.shape
    quarter, half = rows // RING, w_out.shape[1] // 2
    even, odd = me ^ 1, RING - 1 - me
    parts = attended.reshape(RING, quarter, depth)

    def pick(one, two):
        return jnp.concatenate(
            [
                lax.dynamic_index_in_dim(parts, one, 0, keepdims=False),
                lax.dynamic_index_in_dim(parts, two, 0, keepdims=False),
            ],
            axis=0,
        )

    across = (me + 2) % RING
    got_even = lax.ppermute(pick(even, across), "kvh", EVEN)
    got_odd = lax.ppermute(pick(odd, across), "kvh", ODD)

    def times(rows, w):
        return jnp.dot(rows, w, preferred_element_type=jnp.float32)

    def part(index):
        return lax.dynamic_index_in_dim(parts, index, 0, keepdims=False)

    sent_first = times(part(odd), w_out[:, :half]) + times(got_even[quarter:], w_near[0])
    sent_second = times(part(even), w_out[:, half:]) + times(got_odd[quarter:], w_near[1])
    other_first = lax.ppermute(sent_first.astype(jnp.bfloat16), "kvh", ODD)
    other_second = lax.ppermute(sent_second.astype(jnp.bfloat16), "kvh", EVEN)
    kept = times(part(me), w_out)
    kept_first = kept[:, :half] + times(got_even[:quarter], w_near[0])
    kept_second = kept[:, half:] + times(got_odd[:quarter], w_near[1])
    return jnp.concatenate(
        [
            (kept_first + other_first.astype(jnp.float32)).astype(jnp.bfloat16),
            (kept_second + other_second.astype(jnp.float32)).astype(jnp.bfloat16),
        ],
        axis=1,
    )


def after(value, *others):
    return lax.optimization_barrier((value, *others))[0]


def local(tokens, norm_gain, w_query, w_key, w_value, w_out, picks):
    me, block_index = lax.axis_index("kvh"), lax.axis_index("ctx")
    ctx_count = lax.axis_size("ctx")
    block_len = tokens.shape[0]
    half = block_len // 2
    chosen = picks[0, 0]

    wanted = lax.all_to_all(
        jnp.broadcast_to(chosen[None, None, 1:], (ctx_count, 1, 2)), "ctx", 0, 0
    ).reshape(ctx_count * 2)

    width = tokens.shape[1]
    from_left = lax.ppermute(tokens, "kvh", RIGHT)
    from_right = lax.ppermute(tokens, "kvh", LEFT)
    positions = block_index * block_len + jnp.arange(block_len, dtype=jnp.int32)
    cosine, sine = turns(positions)
    def weights(w, place):
        start = place % RING * width
        rows = lax.dynamic_slice_in_dim(w, start, width, 0)
        return (rows * lax.dynamic_slice_in_dim(norm_gain, start, width, 0)[:, None]).astype(jnp.bfloat16)

    def times(rows, w):
        return jnp.dot(rows, w, preferred_element_type=jnp.float32)

    w_kv = jnp.concatenate([w_key, w_value], axis=1)
    kv_own = times(tokens, weights(w_kv, me))
    kv_weights = [weights(w_kv, me + step) for step in (3, 1, 2)]
    from_left, from_right, wanted, cosine, kv_own, kv_weights = lax.optimization_barrier(
        (from_left, from_right, wanted, cosine, kv_own, kv_weights)
    )
    upper = lax.ppermute(from_left[:half], "kvh", RIGHT)
    lower = lax.ppermute(from_right[half:], "kvh", LEFT)

    def project(own, left, right, across):
        sofar = own + times(from_left, left) + times(from_right, right)
        return sofar + jnp.concatenate([times(upper, across), times(lower, across)], axis=0)

    def squares(rows):
        return jnp.sum(jnp.square(rows.astype(jnp.float32)), axis=1, keepdims=True)

    square_sum = squares(tokens) + squares(from_left) + squares(from_right)
    square_sum += jnp.concatenate([squares(upper), squares(lower)], axis=0)
    scale = lax.rsqrt(square_sum / (RING * width) + 1e-05)

    kv = project(kv_own, *kv_weights) * scale
    key_rows = rotate_pairs(kv[:, None, :HD], cosine, sine)[:, 0].astype(jnp.bfloat16)
    own = jnp.concatenate([key_rows, kv[:, HD:].astype(jnp.bfloat16)], axis=0)
    held = lax.all_to_all(own.reshape(ctx_count, -1, HD), "ctx", 0, 0)
    before = lax.ppermute(own, "ctx", [(i, i + 1) for i in range(ctx_count - 1)])
    got = lax.all_to_all(route(wanted, held).reshape(ctx_count, 2, -1, HD), "ctx", 0, 0)

    mid = w_out.shape[1] // 2
    passed = after(w_out, from_left)
    front, back = after(passed[:, :mid], upper, lower), after(passed[:, mid:], upper, lower)
    w_near = lax.ppermute(front, "kvh", EVEN), lax.ppermute(back, "kvh", ODD)

    w_late = after(w_query, from_left)
    queries = (project(
        times(tokens, weights(w_late, me)), *(weights(w_late, me + step) for step in (3, 1, 2))
    ) * scale).reshape(block_len, -1, HD)
    queries = rotate_pairs(queries, cosine, sine).astype(jnp.bfloat16).reshape(block_len, -1)
    flags = (chosen < block_index).astype(jnp.int32)
    sums, stats = attend_near(flags, queries, own, before)
    attended = attend_far(flags, queries, got, sums, stats)
    return project_out(attended, w_out, w_near, me)


def solution(mesh):
    in_specs = (
        P("ctx", "kvh"),
        P(),
        P(None, "kvh"),
        P(None, "kvh"),
        P(None, "kvh"),
        P("kvh", None),
        P("ctx", "kvh", None),
    )
    out_specs = P(("ctx", "kvh"), None)
    return jax.shard_map(local, mesh=mesh, in_specs=in_specs, out_specs=out_specs, check_vma=False)
```

profile of v0, /device:TPU:1, one launch (start us, length us, event | category | flops | bytes accessed | tf_op | source)
XLA Modules:
  0.0 142.0 jit_solution(6978153289926680246)
XLA Ops:
  0.0 2.0 %collective-permute-start = (bf16[512,1024]{1,0:T(8,128)(2,1)}, bf16[512,1024]{1,0:T(8,128)(2,1)S(1)}, u32[]{:S(2)}, u32[]{:S(2)}) collective-permute-start(bf16[512,1024]{1,0:T(8,128)(2,1)} %param.7), channel_id=1, source_target_pairs={{0,1},{1,2},{2,3},{3,0},{4,5},{5,6},{6,7},{7,4},{8,9},{9,10},{10,1... | collective-permute-start | bytes 3145736 | tf_op jit(solution)/shard_map/ppermute | solution.py:224
  2.0 1.4 collective-permute-start.1
  4.8 13.0 %all-to-all-start = ((s32[64,1,2]{2,1,0:T(1,128)}), s32[64,1,2]{2,1,0:T(1,128)S(1)}, u32[]{:S(2)}, u32[]{:S(2)}) async-start(s32[64,1,2]{2,1,0:T(1,128)} %broadcast_in_dim.9), calls=%async_computation | async-start | bytes 65536 | tf_op jit(solution)/shard_map/all_to_all | solution.py:219
  17.8 2.3 %constant_dynamic-update-slice_fusion.1 = bf16[4096,256]{1,0:T(8,128)(2,1)} fusion(bf16[4096,128]{1,0:T(8,128)(2,1)} %param.10), kind=kLoop, calls=%fused_computation.77 | loop fusion | bytes 2097152
  21.3 1.8 %multiply_sine_fusion = (f32[512,64]{1,0:T(8,128)}, f32[512,64]{1,0:T(8,128)S(1)}) fusion(f32[64]{0:T(128)S(1)} %multiply_power_fusion, f32[512]{0:T(512)S(1)} %add_convert_fusion.1), kind=kLoop, calls=%fused_computation.49 | loop fusion | flops 32768 | bytes 264448 | tf_op jit(solution)/shard_map/sin | solution.py:18
  23.1 2.5 %convolution_bitcast_fusion.1 = f32[512,256]{1,0:T(8,128)} fusion(bf16[512,1024]{1,0:T(8,128)(2,1)S(1)} %copy-done.12, f32[1024]{0:T(1024)S(1)} %get-tuple-element.51, bf16[4096,256]{1,0:T(8,128)(2,1)} %constant_dynamic-update-slice_fusion, s32[]{:T(128)S(6)} %select_n.70), kind=kOutput, calls=%fused_computation.26 | convolution fusion | flops 269221888 | bytes 2101252 | tf_op jit(solution)/shard_map/dot_general | solution.py:234
  25.6 1.4 %multiply_convert_fusion.7 = (bf16[1024,256]{1,0:T(8,128)(2,1)S(1)}, bf16[1024,256]{1,0:T(8,128)(2,1)}, bf16[1024,256]{1,0:T(8,128)(2,1)}) fusion(f32[1024]{0:T(1024)S(1)} %get-tuple-element.49, bf16[4096,256]{1,0:T(8,128)(2,1)S(1)} %copy-done.1, s32[]{:T(128)S(6)} %select_n.76, f32[1024]{0:T(1024)S(1)} %get-tuple-element.52, s32[]{:T(128)S(6)} %select_n.74, ...), kind=kLoop, calls=%fused_computation.39 | loop fusion | flops 2359296 | bytes 3158028 | tf_op jit(solution)/shard_map/convert_element_type | solution.py:231
  28.9 1.3 collective-permute-start.3
  30.6 4.8 %fusion.47 = (bf16[512,2048]{1,0:T(8,128)(2,1)}, bf16[512,2048]{1,0:T(8,128)(2,1)}) fusion(bf16[512,4096]{1,0:T(8,128)(2,1)} %param.12), kind=kLoop, calls=%fused_computation.94 | loop fusion | bytes 8388608 | tf_op jit(solution)/shard_map/slice | solution.py:265
  36.3 3.1 %fusion.13 = f32[512,512]{0,1:T(8,128)} fusion(bf16[512,1024]{1,0:T(8,128)(2,1)S(1)} %collective-permute-done.1, f32[1024]{0:T(1024)S(1)} %get-tuple-element.52, bf16[4096,512]{1,0:T(8,128)(2,1)} %param.9, s32[]{:T(128)S(6)} %select_n.74), kind=kOutput, calls=%fused_computation.27 | convolution fusion | flops 538443776 | bytes 3149828 | tf_op jit(solution)/shard_map/dot_general | solution.py:234
  39.4 2.6 %collective-permute-done.3 = bf16[256,1024]{1,0:T(8,128)(2,1)S(1)} collective-permute-done((bf16[256,1024]{1,0:T(8,128)(2,1)S(1)}, bf16[256,1024]{1,0:T(8,128)(2,1)S(1)}, u32[]{:S(2)}, u32[]{:S(2)}) %collective-permute-start.3) | collective-permute-done | bytes 524320 | tf_op jit(solution)/shard_map/ppermute | solution.py:243
  42.2 2.1 %collective-permute-done.2 = bf16[256,1024]{1,0:T(8,128)(2,1)S(1)} collective-permute-done((bf16[256,1024]{1,0:T(8,128)(2,1)S(1)}, bf16[256,1024]{1,0:T(8,128)(2,1)S(1)}, u32[]{:S(2)}, u32[]{:S(2)}) %collective-permute-start.2) | collective-permute-done | bytes 524320 | tf_op jit(solution)/shard_map/ppermute | solution.py:242
  47.5 11.9 %all-to-all-start.1 = ((bf16[64,16,128]{2,1,0:T(8,128)(2,1)}), bf16[64,16,128]{2,1,0:T(8,128)(2,1)S(1)}, u32[]{:S(2)}, u32[]{:S(2)}) async-start(bf16[64,16,128]{2,1,0:T(8,128)(2,1)} %bitcast.8), calls=%async_computation.1 | async-start | bytes 524288 | tf_op jit(solution)/shard_map/all_to_all | solution.py:259
  59.5 3.7 %convolution_bitcast_fusion = f32[512,512]{0,1:T(8,128)} fusion(bf16[512,1024]{1,0:T(8,128)(2,1)} %param.7, f32[1024]{0:T(1024)S(1)} %get-tuple-element.51, bf16[4096,512]{1,0:T(8,128)(2,1)} %param.9, s32[]{:T(128)S(6)} %select_n.70), kind=kOutput, calls=%fused_computation.23 | convolution fusion | flops 538443776 | bytes 3149828 | tf_op jit(solution)/shard_map/dot_general | solution.py:234
  63.2 3.5 %collective-permute-start.4 = (bf16[1024,128]{1,0:T(8,128)(2,1)}, bf16[1024,128]{1,0:T(8,128)(2,1)S(1)}, u32[]{:S(2)}, u32[]{:S(2)}) collective-permute-start(bf16[1024,128]{1,0:T(8,128)(2,1)} %pad_maximum_fusion.4.own_ref), channel_id=1, source_target_pairs={{0,4},{4,8},{8,12},{12,16},{16,20},{20,24},{24,28},{28,32},{32,36}... | collective-permute-start | bytes 786440 | tf_op jit(solution)/shard_map/ppermute | solution.py:260
  67.0 2.8 %fusion.24 = f32[256,512]{0,1:T(8,128)} fusion(bf16[256,1024]{1,0:T(8,128)(2,1)S(1)} %copy-done.8, f32[1024]{0:T(1024)S(1)} %get-tuple-element.49, bf16[4096,512]{1,0:T(8,128)(2,1)} %param.9, s32[]{:T(128)S(6)} %select_n.76), kind=kOutput, calls=%fused_computation.52 | convolution fusion | flops 270008320 | bytes 2101252 | tf_op jit(solution)/shard_map/dot_general | solution.py:234
  69.7 2.8 %fusion.23 = f32[256,512]{0,1:T(8,128)} fusion(bf16[256,1024]{1,0:T(8,128)(2,1)S(1)} %copy-done.6, f32[1024]{0:T(1024)S(1)} %get-tuple-element.49, bf16[4096,512]{1,0:T(8,128)(2,1)} %param.9, s32[]{:T(128)S(6)} %select_n.76), kind=kOutput, calls=%fused_computation.51 | convolution fusion | flops 270008320 | bytes 2101252 | tf_op jit(solution)/shard_map/dot_general | solution.py:234
  72.7 1.4 %route.1 = bf16[128,16,128]{2,1,0:T(8,128)(2,1)} custom-call(s32[128]{0:T(128)S(1)} %reshape.129.wanted_ref, bf16[64,16,128]{2,1,0:T(8,128)(2,1)S(1)} %all-to-all-done.1.held_ref), custom_call_target="tpu_custom_call" | custom-call | flops 1048576 | bytes 4194304 | tf_op jit(solution)/shard_map/route/pallas_call | solution.py:129
  74.1 9.4 %all-to-all-start.2 = ((bf16[64,2,16,128]{3,2,1,0:T(8,128)(2,1)}), bf16[64,2,16,128]{3,2,1,0:T(8,128)(2,1)S(1)}, u32[]{:S(2)}, u32[]{:S(2)}) async-start(bf16[64,2,16,128]{3,2,1,0:T(8,128)(2,1)} %bitcast.9), calls=%async_computation.2 | async-start | bytes 1048576 | tf_op jit(solution)/shard_map/all_to_all | solution.py:261
  83.6 2.7 %fusion.12 = f32[512,512]{0,1:T(8,128)S(1)} fusion(f32[512,512]{0,1:T(8,128)S(1)} %copy-done.13, f32[512,512]{0,1:T(8,128)} %convolution_bitcast_fusion, bf16[512,1024]{1,0:T(8,128)(2,1)S(1)} %collective-permute-done, f32[256,512]{0,1:T(8,128)} %fusion.23, f32[256,512]{0,1:T(8,128)S(1)} %copy-done.15, f32[1024]{0:T(1024)S(1)} %get-tuple-element.50, ...), kind=kOutput, calls=%fused_computation.25 | convolution fusion | flops 539754496 | bytes 6297604 | tf_op jit(solution)/shard_map/dot_general | solution.py:234
  87.5 1.4 %copy.35 = f32[512,4,64]{2,1,0:T(4,128)S(1)} copy(f32[512,4,64]{0,2,1:T(8,128)} %get-tuple-element.40) | data formatting | bytes 1048576
  90.4 4.5 %attend_near.1 = (f32[2048,128]{1,0:T(8,128)S(1)}, f32[2048,128]{1,0:T(8,128)S(1)}) custom-call(s32[3]{0:T(128)S(1)} %fusion.46.flag_ref, bf16[512,512]{1,0:T(8,128)(2,1)S(1)} %bitcast.63, bf16[1024,128]{1,0:T(8,128)(2,1)} %pad_maximum_fusion.4.own_ref, bf16[1024,128]{1,0:T(8,128)(2,1)S(1)} %collective-permute-done.4.before_ref), custom_call_target="tpu_custom_call" | custom-call | flops 1073741824 | bytes 4194304 | tf_op jit(solution)/shard_map/attend_near/pallas_call | solution.py:129
  94.9 6.4 %all-to-all-done.2.got_ref = bf16[64,2,16,128]{3,2,1,0:T(8,128)(2,1)S(1)} async-done(((bf16[64,2,16,128]{3,2,1,0:T(8,128)(2,1)}), bf16[64,2,16,128]{3,2,1,0:T(8,128)(2,1)S(1)}, u32[]{:S(2)}, u32[]{:S(2)}) %all-to-all-start.2) | async-done | bytes 524320 | tf_op jit(solution)/shard_map/all_to_all | solution.py:261
  101.3 5.2 %attend_far.1 = bf16[512,512]{1,0:T(8,128)(2,1)S(1)} custom-call(s32[3]{0:T(128)S(1)} %fusion.46.flag_ref, bf16[512,512]{1,0:T(8,128)(2,1)S(1)} %bitcast.64, bf16[64,2,16,128]{3,2,1,0:T(8,128)(2,1)S(1)} %all-to-all-done.2.got_ref, f32[2048,128]{1,0:T(8,128)S(1)} %get-tuple-element.28.sums_ref, f32[2048,128]{1,0:T(8,128)S(1)} %get-tuple-element.29.stats_ref), custom_call_target="tpu_custom_call" | custom-call | flops 1073741824 | bytes 4194304 | tf_op jit(solution)/shard_map/attend_far/pallas_call | solution.py:129
  106.5 1.4 collective-permute-start.5
  107.9 2.1 %collective-permute-start.8 = (bf16[256,512]{1,0:T(8,128)(2,1)S(1)}, bf16[256,512]{1,0:T(8,128)(2,1)S(1)}, u32[]{:S(2)}, u32[]{:S(2)}) collective-permute-start(bf16[256,512]{1,0:T(8,128)(2,1)S(1)} %get-tuple-element.48), channel_id=1, source_target_pairs={{0,3},{1,2},{2,1},{3,0},{4,7},{5,6},{6,5},{7,4},{8,11},{9,10},{10,... | collective-permute-start | bytes 786440 | tf_op jit(solution)/shard_map/ppermute | solution.py:184
  110.9 8.7 %collective-permute-done.5 = bf16[256,512]{1,0:T(8,128)(2,1)S(1)} collective-permute-done((bf16[256,512]{1,0:T(8,128)(2,1)S(1)}, bf16[256,512]{1,0:T(8,128)(2,1)S(1)}, u32[]{:S(2)}, u32[]{:S(2)}) %collective-permute-start.5) | collective-permute-done | bytes 262176 | tf_op jit(solution)/shard_map/ppermute | solution.py:183
  119.6 2.1 %fusion.3 = bf16[128,2048]{1,0:T(8,128)(2,1)S(1)} fusion(f32[128,2048]{1,0:T(8,128)S(1)} %fusion.8, bf16[512,2048]{1,0:T(8,128)(2,1)} %collective-permute-done.6, bf16[256,512]{1,0:T(8,128)(2,1)S(1)} %collective-permute-done.5), kind=kOutput, calls=%fused_computation.7 | convolution fusion | flops 268959744 | bytes 3801088 | tf_op jit(solution)/shard_map/dot_general | solution.py:187
  121.9 2.1 %fusion.5 = bf16[128,2048]{1,0:T(8,128)(2,1)S(1)} fusion(f32[128,2048]{1,0:T(8,128)S(1)} %fusion.6, bf16[512,2048]{1,0:T(8,128)(2,1)} %collective-permute-done.9, bf16[256,512]{1,0:T(8,128)(2,1)S(1)} %collective-permute-done.8), kind=kOutput, calls=%fused_computation.9 | convolution fusion | flops 268959744 | bytes 3801088 | tf_op jit(solution)/shard_map/dot_general | solution.py:187
  124.8 11.9 %collective-permute-done.7 = bf16[128,2048]{1,0:T(8,128)(2,1)S(1)} collective-permute-done((bf16[128,2048]{1,0:T(8,128)(2,1)S(1)}, bf16[128,2048]{1,0:T(8,128)(2,1)S(1)}, u32[]{:S(2)}, u32[]{:S(2)}) %collective-permute-start.7) | collective-permute-done | bytes 524320 | tf_op jit(solution)/shard_map/ppermute | solution.py:194
  136.7 2.1 %fusion.2 = bf16[128,2048]{1,0:T(8,128)(2,1)S(1)} fusion(bf16[512,2048]{1,0:T(8,128)(2,1)} %collective-permute-done.6, f32[128,4096]{1,0:T(8,128)S(1)} %fusion.33, bf16[128,2048]{1,0:T(8,128)(2,1)S(1)} %collective-permute-done.7, bf16[256,512]{1,0:T(8,128)(2,1)S(1)} %collective-permute-done.5), kind=kOutput, calls=%fused_computation.6 | convolution fusion | flops 269484032 | bytes 4325376 | tf_op jit(solution)/shard_map/dot_general | solution.py:187
  138.8 2.1 %fusion.4 = bf16[128,2048]{1,0:T(8,128)(2,1)S(1)} fusion(bf16[512,2048]{1,0:T(8,128)(2,1)} %collective-permute-done.9, f32[128,4096]{1,0:T(8,128)S(1)} %fusion.33, bf16[128,2048]{1,0:T(8,128)(2,1)S(1)} %collective-permute-done.10, bf16[256,512]{1,0:T(8,128)(2,1)S(1)} %collective-permute-done.8), kind=kOutput, calls=%fused_computation.8 | convolution fusion | flops 269484032 | bytes 4325376 | tf_op jit(solution)/shard_map/dot_general | solution.py:187
  (87 shorter events, 15.0 us)
Async XLA Ops:
  0.0 20.1 %copy-start.17 = (s32[1,1,3]{2,1,0:T(1,128)S(1)}, s32[1,1,3]{2,1,0:T(1,128)}, u32[]{:S(2)}) copy-start(s32[1,1,3]{2,1,0:T(1,128)} %param.13) | copy-start | bytes 40
  0.0 20.2 %copy-start.11 = (bf16[4096,128]{1,0:T(8,128)(2,1)S(1)}, bf16[4096,128]{1,0:T(8,128)(2,1)}, u32[]{:S(2)}) copy-start(bf16[4096,128]{1,0:T(8,128)(2,1)} %param.11) | copy-start | bytes 3145732
  0.0 28.8 %collective-permute-start = (bf16[512,1024]{1,0:T(8,128)(2,1)}, bf16[512,1024]{1,0:T(8,128)(2,1)S(1)}, u32[]{:S(2)}, u32[]{:S(2)}) collective-permute-start(bf16[512,1024]{1,0:T(8,128)(2,1)} %param.7), channel_id=1, source_target_pairs={{0,1},{1,2},{2,3},{3,0},{4,5},{5,6},{6,7},{7,4},{8,9},{9,10},{10,1... | collective-permute-start | bytes 3145736 | tf_op jit(solution)/shard_map/ppermute | solution.py:224
  2.0 26.8 %collective-permute-start.1 = (bf16[512,1024]{1,0:T(8,128)(2,1)}, bf16[512,1024]{1,0:T(8,128)(2,1)S(1)}, u32[]{:S(2)}, u32[]{:S(2)}) collective-permute-start(bf16[512,1024]{1,0:T(8,128)(2,1)} %param.7), channel_id=1, source_target_pairs={{0,3},{1,0},{2,1},{3,2},{4,7},{5,4},{6,5},{7,6},{8,11},{9,8},{10,9... | collective-permute-start | bytes 3145736 | tf_op jit(solution)/shard_map/ppermute | solution.py:225
  4.8 22.6 %all-to-all-start = ((s32[64,1,2]{2,1,0:T(1,128)}), s32[64,1,2]{2,1,0:T(1,128)S(1)}, u32[]{:S(2)}, u32[]{:S(2)}) async-start(s32[64,1,2]{2,1,0:T(1,128)} %broadcast_in_dim.9), calls=%async_computation | async-start | bytes 65536 | tf_op jit(solution)/shard_map/all_to_all | solution.py:219
  17.8 3.5 %copy-start.16 = (f32[4096]{0:T(1024)S(1)}, f32[4096]{0:T(1024)}, u32[]{:S(2)}) copy-start(f32[4096]{0:T(1024)} %param.8) | copy-start | bytes 49156
  20.2 2.9 %copy-start.12 = (bf16[512,1024]{1,0:T(8,128)(2,1)S(1)}, bf16[512,1024]{1,0:T(8,128)(2,1)}, u32[]{:S(2)}) copy-start(bf16[512,1024]{1,0:T(8,128)(2,1)} %param.7) | copy-start | bytes 3145732
  21.3 4.3 %copy-start.1 = (bf16[4096,256]{1,0:T(8,128)(2,1)S(1)}, bf16[4096,256]{1,0:T(8,128)(2,1)}, u32[]{:S(2)}) copy-start(bf16[4096,256]{1,0:T(8,128)(2,1)} %constant_dynamic-update-slice_fusion) | copy-start | bytes 6291460
  23.1 22.6 %copy-start.2 = (f32[512,64]{1,0:T(8,128)}, f32[512,64]{1,0:T(8,128)S(1)}, u32[]{:S(2)}) copy-start(f32[512,64]{1,0:T(8,128)S(1)} %get-tuple-element.22) | copy-start | bytes 393220
  28.9 13.1 %collective-permute-start.3 = (bf16[256,1024]{1,0:T(8,128)(2,1)S(1)}, bf16[256,1024]{1,0:T(8,128)(2,1)S(1)}, u32[]{:S(2)}, u32[]{:S(2)}) collective-permute-start(bf16[256,1024]{1,0:T(8,128)(2,1)S(1)} %slice.61), channel_id=1, source_target_pairs={{0,3},{1,0},{2,1},{3,2},{4,7},{5,4},{6,5},{7,6},{8,11},{9,8},{10,9... | collective-permute-start | bytes 1572872 | tf_op jit(solution)/shard_map/ppermute | solution.py:243
  30.3 5.0 %copy-start.9 = (bf16[1024,256]{1,0:T(8,128)(2,1)S(1)}, bf16[1024,256]{1,0:T(8,128)(2,1)}, u32[]{:S(2)}) copy-start(bf16[1024,256]{1,0:T(8,128)(2,1)} %get-tuple-element.25) | copy-start | bytes 1572868
  30.3 14.0 %collective-permute-start.2 = (bf16[256,1024]{1,0:T(8,128)(2,1)S(1)}, bf16[256,1024]{1,0:T(8,128)(2,1)S(1)}, u32[]{:S(2)}, u32[]{:S(2)}) collective-permute-start(bf16[256,1024]{1,0:T(8,128)(2,1)S(1)} %slice.60), channel_id=1, source_target_pairs={{0,1},{1,2},{2,3},{3,0},{4,5},{5,6},{6,7},{7,4},{8,9},{9,10},{10,1... | collective-permute-start | bytes 1572872 | tf_op jit(solution)/shard_map/ppermute | solution.py:242
  39.4 5.7 %copy-start.4 = (bf16[1024,256]{1,0:T(8,128)(2,1)S(1)}, bf16[1024,256]{1,0:T(8,128)(2,1)}, u32[]{:S(2)}) copy-start(bf16[1024,256]{1,0:T(8,128)(2,1)} %get-tuple-element.26) | copy-start | bytes 1572868
  39.4 5.7 %copy-start.14 = (f32[512,256]{1,0:T(8,128)S(1)}, f32[512,256]{1,0:T(8,128)}, u32[]{:S(2)}) copy-start(f32[512,256]{1,0:T(8,128)} %convolution_bitcast_fusion.1) | copy-start | bytes 1572868
  42.0 3.6 %copy-start.5 = (bf16[256,1024]{1,0:T(8,128)(2,1)}, bf16[256,1024]{1,0:T(8,128)(2,1)S(1)}, u32[]{:S(2)}) copy-start(bf16[256,1024]{1,0:T(8,128)(2,1)S(1)} %collective-permute-done.3) | copy-start | bytes 1572868
  44.3 1.3 copy-start.7
  47.5 19.4 %copy-start.8 = (bf16[256,1024]{1,0:T(8,128)(2,1)S(1)}, bf16[256,1024]{1,0:T(8,128)(2,1)}, u32[]{:S(2)}) copy-start(bf16[256,1024]{1,0:T(8,128)(2,1)} %copy-done.7) | copy-start | bytes 1572868
  47.5 25.1 %all-to-all-start.1 = ((bf16[64,16,128]{2,1,0:T(8,128)(2,1)}), bf16[64,16,128]{2,1,0:T(8,128)(2,1)S(1)}, u32[]{:S(2)}, u32[]{:S(2)}) async-start(bf16[64,16,128]{2,1,0:T(8,128)(2,1)} %bitcast.8), calls=%async_computation.1 | async-start | bytes 524288 | tf_op jit(solution)/shard_map/all_to_all | solution.py:259
  59.5 10.3 %copy-start.6 = (bf16[256,1024]{1,0:T(8,128)(2,1)S(1)}, bf16[256,1024]{1,0:T(8,128)(2,1)}, u32[]{:S(2)}) copy-start(bf16[256,1024]{1,0:T(8,128)(2,1)} %copy-done.5) | copy-start | bytes 1572868
  63.2 27.2 %collective-permute-start.4 = (bf16[1024,128]{1,0:T(8,128)(2,1)}, bf16[1024,128]{1,0:T(8,128)(2,1)S(1)}, u32[]{:S(2)}, u32[]{:S(2)}) collective-permute-start(bf16[1024,128]{1,0:T(8,128)(2,1)} %pad_maximum_fusion.4.own_ref), channel_id=1, source_target_pairs={{0,4},{4,8},{8,12},{12,16},{16,20},{20,24},{24,28},{28,32},{32,36}... | collective-permute-start | bytes 786440 | tf_op jit(solution)/shard_map/ppermute | solution.py:260
  66.7 52.9 %collective-permute-start.6 = (bf16[512,2048]{1,0:T(8,128)(2,1)}, bf16[512,2048]{1,0:T(8,128)(2,1)}, u32[]{:S(2)}, u32[]{:S(2)}) collective-permute-start(bf16[512,2048]{1,0:T(8,128)(2,1)} %get-tuple-element.31), channel_id=1, source_target_pairs={{0,1},{1,0},{2,3},{3,2},{4,5},{5,4},{6,7},{7,6},{8,9},{9,8},{10,11... | collective-permute-start | bytes 6291464 | tf_op jit(solution)/shard_map/ppermute | solution.py:266
  66.8 55.0 %collective-permute-start.9 = (bf16[512,2048]{1,0:T(8,128)(2,1)}, bf16[512,2048]{1,0:T(8,128)(2,1)}, u32[]{:S(2)}, u32[]{:S(2)}) collective-permute-start(bf16[512,2048]{1,0:T(8,128)(2,1)} %get-tuple-element.32), channel_id=1, source_target_pairs={{0,3},{1,2},{2,1},{3,0},{4,7},{5,6},{6,5},{7,4},{8,11},{9,10},{10,... | collective-permute-start | bytes 6291464 | tf_op jit(solution)/shard_map/ppermute | solution.py:266
  72.5 11.0 %copy-start.13 = (f32[512,512]{0,1:T(8,128)S(1)}, f32[512,512]{0,1:T(8,128)}, u32[]{:S(2)}) copy-start(f32[512,512]{0,1:T(8,128)} %fusion.13) | copy-start | bytes 3145732
  72.5 11.0 %copy-start.15 = (f32[256,512]{0,1:T(8,128)S(1)}, f32[256,512]{0,1:T(8,128)}, u32[]{:S(2)}) copy-start(f32[256,512]{0,1:T(8,128)} %fusion.24) | copy-start | bytes 1572868
  74.1 27.2 %all-to-all-start.2 = ((bf16[64,2,16,128]{3,2,1,0:T(8,128)(2,1)}), bf16[64,2,16,128]{3,2,1,0:T(8,128)(2,1)S(1)}, u32[]{:S(2)}, u32[]{:S(2)}) async-start(bf16[64,2,16,128]{3,2,1,0:T(8,128)(2,1)} %bitcast.9), calls=%async_computation.2 | async-start | bytes 1048576 | tf_op jit(solution)/shard_map/all_to_all | solution.py:261
  87.1 1.8 %copy-start.3 = (f32[512,64]{1,0:T(8,128)S(1)}, f32[512,64]{1,0:T(8,128)}, u32[]{:S(2)}) copy-start(f32[512,64]{1,0:T(8,128)} %copy-done.2) | copy-start | bytes 393220
  87.1 1.9 %copy-start.10 = (f32[512,64]{1,0:T(8,128)S(1)}, f32[512,64]{1,0:T(8,128)}, u32[]{:S(2)}) copy-start(f32[512,64]{1,0:T(8,128)} %get-tuple-element.53) | copy-start | bytes 393220
  101.3 8.7 %copy-start = (bf16[512,4096]{1,0:T(8,128)(2,1)S(1)}, bf16[512,4096]{1,0:T(8,128)(2,1)}, u32[]{:S(2)}) copy-start(bf16[512,4096]{1,0:T(8,128)(2,1)} %param.12) | copy-start | bytes 12582916
  106.5 13.1 %collective-permute-start.5 = (bf16[256,512]{1,0:T(8,128)(2,1)S(1)}, bf16[256,512]{1,0:T(8,128)(2,1)S(1)}, u32[]{:S(2)}, u32[]{:S(2)}) collective-permute-start(bf16[256,512]{1,0:T(8,128)(2,1)S(1)} %get-tuple-element.47), channel_id=1, source_target_pairs={{0,1},{1,0},{2,3},{3,2},{4,5},{5,4},{6,7},{7,6},{8,9},{9,8},{10,11... | collective-permute-start | bytes 786440 | tf_op jit(solution)/shard_map/ppermute | solution.py:183
  107.9 13.9 %collective-permute-start.8 = (bf16[256,512]{1,0:T(8,128)(2,1)S(1)}, bf16[256,512]{1,0:T(8,128)(2,1)S(1)}, u32[]{:S(2)}, u32[]{:S(2)}) collective-permute-start(bf16[256,512]{1,0:T(8,128)(2,1)S(1)} %get-tuple-element.48), channel_id=1, source_target_pairs={{0,3},{1,2},{2,1},{3,0},{4,7},{5,6},{6,5},{7,4},{8,11},{9,10},{10,... | collective-permute-start | bytes 786440 | tf_op jit(solution)/shard_map/ppermute | solution.py:184
  121.7 15.0 %collective-permute-start.7 = (bf16[128,2048]{1,0:T(8,128)(2,1)S(1)}, bf16[128,2048]{1,0:T(8,128)(2,1)S(1)}, u32[]{:S(2)}, u32[]{:S(2)}) collective-permute-start(bf16[128,2048]{1,0:T(8,128)(2,1)S(1)} %fusion.3), channel_id=1, source_target_pairs={{0,3},{1,2},{2,1},{3,0},{4,7},{5,6},{6,5},{7,4},{8,11},{9,10},{10,... | collective-permute-start | bytes 1572872 | tf_op jit(solution)/shard_map/ppermute | solution.py:194
  123.9 14.9 %collective-permute-start.10 = (bf16[128,2048]{1,0:T(8,128)(2,1)S(1)}, bf16[128,2048]{1,0:T(8,128)(2,1)S(1)}, u32[]{:S(2)}, u32[]{:S(2)}) collective-permute-start(bf16[128,2048]{1,0:T(8,128)(2,1)S(1)} %fusion.5), channel_id=1, source_target_pairs={{0,1},{1,0},{2,3},{3,2},{4,5},{5,4},{6,7},{7,6},{8,9},{9,8},{10,11... | collective-permute-start | bytes 1572872 | tf_op jit(solution)/shard_map/ppermute | solution.py:195
where the time goes:
time: 143 us; the launch traced here: 142 us
  starting transfers between devices  46.9 us (33%)
  waiting for transfers between devices  31.8 us (22%)
  matrix products  29.1 us (20%)
  local copies, waits for them, and re-layouts  13.2 us (9%)
  Pallas kernels  11.1 us (8%)
  other arithmetic  9.38 us (7%)
    dot_general x17, matrix products, times(): return jnp.dot(rows, w, preferred_element_type=jnp.float32)  29.1 us
    all_to_all x1, starting transfers between devices, local(): lax.all_to_all(jnp.broadcast_to(chosen[None, None, 1:], (ctx_count, 1, 2)...  13 us
    all_to_all x1, starting transfers between devices, local(): held = lax.all_to_all(own.reshape(ctx_count, -1, HD), 'ctx', 0, 0)  11.9 us
    ppermute x1, waiting for transfers between devices, project_out(): other_first = lax.ppermute(sent_first.astype(jnp.bfloat16), 'kvh', ODD)  11.9 us
    pallas_call x3, Pallas kernels, call(): pl.pallas_call(kernel, out_shape=out_shape, in_specs=[SMEM] + [VMEM] * (l...  11.1 us
    all_to_all x1, starting transfers between devices, local(): lax.all_to_all(route(wanted, held).reshape(ctx_count, 2, -1, HD), 'ctx',...  9.45 us
    ppermute x1, waiting for transfers between devices, project_out(): got_even = lax.ppermute(pick(even, across), 'kvh', EVEN)  8.71 us
    all_to_all x1, waiting for transfers between devices, local(): lax.all_to_all(route(wanted, held).reshape(ctx_count, 2, -1, HD), 'ctx',...  6.37 us
  transfers between devices with their start and end apart: 14, of which 6 were waited for; matrix products, arithmetic and copies ran while one was open for 32% of the time, Pallas kernels for 8%

commit v1 on v0

--- a/solution.py
+++ b/solution.py
@@ -186,20 +186,14 @@
     def times(rows, w):
         return jnp.dot(rows, w, preferred_element_type=jnp.float32)
 
-    def part(index):
-        return lax.dynamic_index_in_dim(parts, index, 0, keepdims=False)
-
-    sent_first = times(part(odd), w_out[:, :half]) + times(got_even[quarter:], w_near[0])
-    sent_second = times(part(even), w_out[:, half:]) + times(got_odd[quarter:], w_near[1])
-    other_first = lax.ppermute(sent_first.astype(jnp.bfloat16), "kvh", ODD)
-    other_second = lax.ppermute(sent_second.astype(jnp.bfloat16), "kvh", EVEN)
-    kept = times(part(me), w_out)
-    kept_first = kept[:, :half] + times(got_even[:quarter], w_near[0])
-    kept_second = kept[:, half:] + times(got_odd[:quarter], w_near[1])
+    sums_first = times(pick(me, odd), w_out[:, :half]) + times(got_even, w_near[0])
+    other_first = lax.ppermute(sums_first[quarter:].astype(jnp.bfloat16), "kvh", ODD)
+    sums_second = times(pick(me, even), w_out[:, half:]) + times(got_odd, w_near[1])
+    other_second = lax.ppermute(sums_second[quarter:].astype(jnp.bfloat16), "kvh", EVEN)
     return jnp.concatenate(
         [
-            (kept_first + other_first.astype(jnp.float32)).astype(jnp.bfloat16),
-            (kept_second + other_second.astype(jnp.float32)).astype(jnp.bfloat16),
+            (sums_first[:quarter] + other_first.astype(jnp.float32)).astype(jnp.bfloat16),
+            (sums_second[:quarter] + other_second.astype(jnp.float32)).astype(jnp.bfloat16),
         ],
         axis=1,
     )

time: 143 us -> 141 us (0.986)
  matrix products: 29.1 us -> 23.6 us
  starting transfers between devices: 46.9 us -> 51.3 us
    dot_general x17 -> x14, matrix products: 29.1 us -> 23.6 us  [times(): return jnp.dot(rows, w, preferred_element_type=jnp.float32)]
    ppermute x2, starting transfers between devices: 0.25 us -> 3.19 us  [local(): w_near = (lax.ppermute(front, 'kvh', EVEN), lax.ppermute(back, 'kvh', ODD))]
    ppermute x2, starting transfers between devices: 0.25 us -> 3.18 us  [the longest x1 3.09 us: project_out(): lax.ppermute(sums_first[quarter:].astype(jnp.bfloat16), 'kvh', ODD)]
    ppermute x1, waiting for transfers between devices: 2.57 us -> 0.9 us  [local(): lower = lax.ppermute(from_right[half:], 'kvh', LEFT)]
    ppermute x1, starting transfers between devices: 2.07 us -> 0.61 us  [project_out(): got_odd = lax.ppermute(pick(odd, across), 'kvh', ODD)]
    ppermute x2, waiting for transfers between devices: 11.9 us -> 13.4 us  [the longest x1 9.14 us: project_out(): lax.ppermute(sums_first[quarter:].astype(jnp.bfloat16), 'kvh', ODD)]
    unnamed x40 -> x36, local copies, waits for them, and re-layouts: 4.29 us -> 4.55 us
  transfers between devices with their start and end apart: 14 -> 14, of which waited for: 6 -> 7; matrix products, arithmetic and copies ran while one was open for 32% -> 30% of each run, Pallas kernels for 8% -> 8%
where the time goes in v1:
time: 141 us; the launch traced here: 140 us
  starting transfers between devices  51.3 us (36%)
  waiting for transfers between devices  30.6 us (22%)
  matrix products  23.6 us (17%)
  local copies, waits for them, and re-layouts  13.6 us (10%)
  Pallas kernels  11.1 us (8%)
  other arithmetic  9.49 us (7%)
    dot_general x14, matrix products, times(): return jnp.dot(rows, w, preferred_element_type=jnp.float32)  23.6 us
    all_to_all x1, starting transfers between devices, local(): lax.all_to_all(jnp.broadcast_to(chosen[None, None, 1:], (ctx_count, 1, 2)...  13 us
    all_to_all x1, starting transfers between devices, local(): held = lax.all_to_all(own.reshape(ctx_count, -1, HD), 'ctx', 0, 0)  11.2 us
    pallas_call x3, Pallas kernels, call(): pl.pallas_call(kernel, out_shape=out_shape, in_specs=[SMEM] + [VMEM] * (l...  11.1 us
    all_to_all x1, starting transfers between devices, local(): lax.all_to_all(route(wanted, held).reshape(ctx_count, 2, -1, HD), 'ctx',...  9.58 us
    ppermute x1, waiting for transfers between devices, project_out(): lax.ppermute(sums_first[quarter:].astype(jnp.bfloat16), 'kvh', ODD)  9.14 us
    ppermute x1, waiting for transfers between devices, project_out(): got_even = lax.ppermute(pick(even, across), 'kvh', EVEN)  8.77 us
    all_to_all x1, waiting for transfers between devices, local(): lax.all_to_all(route(wanted, held).reshape(ctx_count, 2, -1, HD), 'ctx',...  6.15 us
  transfers between devices with their start and end apart: 14, of which 7 were waited for; matrix products, arithmetic and copies ran while one was open for 30% of the time, Pallas kernels for 8%

profile of v1, /device:TPU:1, one launch (start us, length us, event | category | flops | bytes accessed | tf_op | source)
XLA Modules:
  0.0 140.2 jit_solution(441766660374224920)
XLA Ops:
  0.0 2.0 %collective-permute-start = (bf16[512,1024]{1,0:T(8,128)(2,1)}, bf16[512,1024]{1,0:T(8,128)(2,1)S(1)}, u32[]{:S(2)}, u32[]{:S(2)}) collective-permute-start(bf16[512,1024]{1,0:T(8,128)(2,1)} %param.7), channel_id=1, source_target_pairs={{0,1},{1,2},{2,3},{3,0},{4,5},{5,6},{6,7},{7,4},{8,9},{9,10},{10,1... | collective-permute-start | bytes 3145736 | tf_op jit(solution)/shard_map/ppermute | solution.py:218
  2.0 1.4 collective-permute-start.1
  4.8 13.0 %all-to-all-start = ((s32[64,1,2]{2,1,0:T(1,128)}), s32[64,1,2]{2,1,0:T(1,128)S(1)}, u32[]{:S(2)}, u32[]{:S(2)}) async-start(s32[64,1,2]{2,1,0:T(1,128)} %broadcast_in_dim.9), calls=%async_computation | async-start | bytes 65536 | tf_op jit(solution)/shard_map/all_to_all | solution.py:213
  17.8 2.3 %constant_dynamic-update-slice_fusion.1 = bf16[4096,256]{1,0:T(8,128)(2,1)} fusion(bf16[4096,128]{1,0:T(8,128)(2,1)} %param.10), kind=kLoop, calls=%fused_computation.73 | loop fusion | bytes 2097152
  20.2 1.1 constant_dynamic-update-slice_fusion
  21.3 1.8 %multiply_sine_fusion = (f32[512,64]{1,0:T(8,128)}, f32[512,64]{1,0:T(8,128)S(1)}) fusion(f32[64]{0:T(128)S(1)} %multiply_power_fusion, f32[512]{0:T(512)S(1)} %add_convert_fusion.1), kind=kLoop, calls=%fused_computation.47 | loop fusion | flops 32768 | bytes 264448 | tf_op jit(solution)/shard_map/sin | solution.py:18
  23.1 1.7 %convolution_bitcast_fusion.1 = f32[512,256]{1,0:T(8,128)S(1)} fusion(bf16[512,1024]{1,0:T(8,128)(2,1)S(1)} %copy-done.12, f32[1024]{0:T(1024)S(1)} %get-tuple-element.52, bf16[4096,256]{1,0:T(8,128)(2,1)} %constant_dynamic-update-slice_fusion, s32[]{:T(128)S(6)} %select_n.71), kind=kOutput, calls=%fused_computation.18 | convolution fusion | flops 269221888 | bytes 2101252 | tf_op jit(solution)/shard_map/dot_general | solution.py:228
  24.8 1.4 %multiply_convert_fusion.7 = (bf16[1024,256]{1,0:T(8,128)(2,1)S(1)}, bf16[1024,256]{1,0:T(8,128)(2,1)}, bf16[1024,256]{1,0:T(8,128)(2,1)}) fusion(f32[1024]{0:T(1024)S(1)} %get-tuple-element.50, bf16[4096,256]{1,0:T(8,128)(2,1)S(1)} %copy-done.1, s32[]{:T(128)S(6)} %select_n.77, f32[1024]{0:T(1024)S(1)} %get-tuple-element.53, s32[]{:T(128)S(6)} %select_n.75, ...), kind=kLoop, calls=%fused_computation.37 | loop fusion | flops 2359296 | bytes 3158028 | tf_op jit(solution)/shard_map/convert_element_type | solution.py:225
  28.7 2.7 %collective-permute-start.3 = (bf16[256,1024]{1,0:T(8,128)(2,1)S(1)}, bf16[256,1024]{1,0:T(8,128)(2,1)S(1)}, u32[]{:S(2)}, u32[]{:S(2)}) collective-permute-start(bf16[256,1024]{1,0:T(8,128)(2,1)S(1)} %slice.57), channel_id=1, source_target_pairs={{0,3},{1,0},{2,1},{3,2},{4,7},{5,4},{6,5},{7,6},{8,11},{9,8},{10,9... | collective-permute-start | bytes 1572872 | tf_op jit(solution)/shard_map/ppermute | solution.py:237
  31.4 4.8 %fusion.39 = (bf16[512,2048]{1,0:T(8,128)(2,1)}, bf16[512,2048]{1,0:T(8,128)(2,1)}) fusion(bf16[512,4096]{1,0:T(8,128)(2,1)} %param.12), kind=kLoop, calls=%fused_computation.91 | loop fusion | bytes 8388608 | tf_op jit(solution)/shard_map/slice | solution.py:259
  37.4 3.3 %convolution_bitcast_fusion = f32[512,512]{0,1:T(8,128)} fusion(bf16[512,1024]{1,0:T(8,128)(2,1)S(1)} %copy-done.13, f32[1024]{0:T(1024)S(1)} %get-tuple-element.52, bf16[4096,512]{1,0:T(8,128)(2,1)} %param.9, s32[]{:T(128)S(6)} %select_n.71), kind=kOutput, calls=%fused_computation.15 | convolution fusion | flops 538443776 | bytes 3149828 | tf_op jit(solution)/shard_map/dot_general | solution.py:228
  44.0 1.0 fusion.24
  45.8 11.2 %all-to-all-start.1 = ((bf16[64,16,128]{2,1,0:T(8,128)(2,1)}), bf16[64,16,128]{2,1,0:T(8,128)(2,1)S(1)}, u32[]{:S(2)}, u32[]{:S(2)}) async-start(bf16[64,16,128]{2,1,0:T(8,128)(2,1)} %bitcast.8), calls=%async_computation.1 | async-start | bytes 524288 | tf_op jit(solution)/shard_map/all_to_all | solution.py:253
  57.0 3.2 %fusion.7 = f32[512,512]{0,1:T(8,128)} fusion(bf16[512,1024]{1,0:T(8,128)(2,1)S(1)} %collective-permute-done.1, f32[1024]{0:T(1024)S(1)} %get-tuple-element.53, bf16[4096,512]{1,0:T(8,128)(2,1)} %param.9, s32[]{:T(128)S(6)} %select_n.75), kind=kOutput, calls=%fused_computation.19 | convolution fusion | flops 538443776 | bytes 3149828 | tf_op jit(solution)/shard_map/dot_general | solution.py:228
  60.2 3.5 %collective-permute-start.4 = (bf16[1024,128]{1,0:T(8,128)(2,1)}, bf16[1024,128]{1,0:T(8,128)(2,1)S(1)}, u32[]{:S(2)}, u32[]{:S(2)}) collective-permute-start(bf16[1024,128]{1,0:T(8,128)(2,1)} %pad_maximum_fusion.8.own_ref), channel_id=1, source_target_pairs={{0,4},{4,8},{8,12},{12,16},{16,20},{20,24},{24,28},{28,32},{32,36}... | collective-permute-start | bytes 786440 | tf_op jit(solution)/shard_map/ppermute | solution.py:254
  64.7 2.2 %collective-permute-start.9 = (bf16[512,2048]{1,0:T(8,128)(2,1)}, bf16[512,2048]{1,0:T(8,128)(2,1)}, u32[]{:S(2)}, u32[]{:S(2)}) collective-permute-start(bf16[512,2048]{1,0:T(8,128)(2,1)} %get-tuple-element.32), channel_id=1, source_target_pairs={{0,3},{1,2},{2,1},{3,0},{4,7},{5,6},{6,5},{7,4},{8,11},{9,10},{10,... | collective-permute-start | bytes 6291464 | tf_op jit(solution)/shard_map/ppermute | solution.py:260
  66.9 2.0 %fusion.20 = f32[256,512]{0,1:T(8,128)S(1)} fusion(bf16[256,1024]{1,0:T(8,128)(2,1)S(1)} %copy-done.6, f32[1024]{0:T(1024)S(1)} %get-tuple-element.50, bf16[4096,512]{1,0:T(8,128)(2,1)} %param.9, s32[]{:T(128)S(6)} %select_n.77), kind=kOutput, calls=%fused_computation.50 | convolution fusion | flops 270008320 | bytes 2101252 | tf_op jit(solution)/shard_map/dot_general | solution.py:228
  68.9 2.8 %fusion.19 = f32[256,512]{0,1:T(8,128)} fusion(bf16[256,1024]{1,0:T(8,128)(2,1)S(1)} %copy-done.8, f32[1024]{0:T(1024)S(1)} %get-tuple-element.50, bf16[4096,512]{1,0:T(8,128)(2,1)} %param.9, s32[]{:T(128)S(6)} %select_n.77), kind=kOutput, calls=%fused_computation.49 | convolution fusion | flops 270008320 | bytes 2101252 | tf_op jit(solution)/shard_map/dot_general | solution.py:228
  71.7 1.4 %route.1 = bf16[128,16,128]{2,1,0:T(8,128)(2,1)} custom-call(s32[128]{0:T(128)S(1)} %reshape.129.wanted_ref, bf16[64,16,128]{2,1,0:T(8,128)(2,1)S(1)} %all-to-all-done.1.held_ref), custom_call_target="tpu_custom_call" | custom-call | flops 1048576 | bytes 4194304 | tf_op jit(solution)/shard_map/route/pallas_call | solution.py:129
  73.2 9.6 %all-to-all-start.2 = ((bf16[64,2,16,128]{3,2,1,0:T(8,128)(2,1)}), bf16[64,2,16,128]{3,2,1,0:T(8,128)(2,1)S(1)}, u32[]{:S(2)}, u32[]{:S(2)}) async-start(bf16[64,2,16,128]{3,2,1,0:T(8,128)(2,1)} %bitcast.9), calls=%async_computation.2 | async-start | bytes 1048576 | tf_op jit(solution)/shard_map/all_to_all | solution.py:255
  82.7 2.9 %fusion.6 = f32[512,512]{0,1:T(8,128)S(1)} fusion(f32[512,512]{0,1:T(8,128)} %fusion.7, f32[512,512]{0,1:T(8,128)} %convolution_bitcast_fusion, bf16[512,1024]{1,0:T(8,128)(2,1)S(1)} %collective-permute-done, f32[256,512]{0,1:T(8,128)} %fusion.19, f32[256,512]{0,1:T(8,128)S(1)} %fusion.20, f32[1024]{0:T(1024)S(1)} %get-tuple-element.51, ...), kind=kOutput, calls=%fused_computation.17 | convolution fusion | flops 539754496 | bytes 6297604 | tf_op jit(solution)/shard_map/dot_general | solution.py:228
  87.0 1.4 %copy.35 = f32[512,4,64]{2,1,0:T(4,128)S(1)} copy(f32[512,4,64]{0,2,1:T(8,128)} %get-tuple-element.40) | data formatting | bytes 1048576
  89.8 4.5 %attend_near.1 = (f32[2048,128]{1,0:T(8,128)S(1)}, f32[2048,128]{1,0:T(8,128)S(1)}) custom-call(s32[3]{0:T(128)S(1)} %fusion.36.flag_ref, bf16[512,512]{1,0:T(8,128)(2,1)S(1)} %bitcast.57, bf16[1024,128]{1,0:T(8,128)(2,1)} %pad_maximum_fusion.8.own_ref, bf16[1024,128]{1,0:T(8,128)(2,1)S(1)} %collective-permute-done.4.before_ref), custom_call_target="tpu_custom_call" | custom-call | flops 1073741824 | bytes 4194304 | tf_op jit(solution)/shard_map/attend_near/pallas_call | solution.py:129
  94.3 6.1 %all-to-all-done.2.got_ref = bf16[64,2,16,128]{3,2,1,0:T(8,128)(2,1)S(1)} async-done(((bf16[64,2,16,128]{3,2,1,0:T(8,128)(2,1)}), bf16[64,2,16,128]{3,2,1,0:T(8,128)(2,1)S(1)}, u32[]{:S(2)}, u32[]{:S(2)}) %all-to-all-start.2) | async-done | bytes 524320 | tf_op jit(solution)/shard_map/all_to_all | solution.py:255
  100.5 5.1 %attend_far.1 = bf16[512,512]{1,0:T(8,128)(2,1)S(1)} custom-call(s32[3]{0:T(128)S(1)} %fusion.36.flag_ref, bf16[512,512]{1,0:T(8,128)(2,1)S(1)} %bitcast.58, bf16[64,2,16,128]{3,2,1,0:T(8,128)(2,1)S(1)} %all-to-all-done.2.got_ref, f32[2048,128]{1,0:T(8,128)S(1)} %get-tuple-element.28.sums_ref, f32[2048,128]{1,0:T(8,128)S(1)} %get-tuple-element.29.stats_ref), custom_call_target="tpu_custom_call" | custom-call | flops 1073741824 | bytes 4194304 | tf_op jit(solution)/shard_map/attend_far/pallas_call | solution.py:129
  107.9 8.8 %collective-permute-done.5 = bf16[256,512]{1,0:T(8,128)(2,1)S(1)} collective-permute-done((bf16[256,512]{1,0:T(8,128)(2,1)S(1)}, bf16[256,512]{1,0:T(8,128)(2,1)S(1)}, u32[]{:S(2)}, u32[]{:S(2)}) %collective-permute-start.5) | collective-permute-done | bytes 262176 | tf_op jit(solution)/shard_map/ppermute | solution.py:183
  116.7 2.4 %convolution_add_fusion.1 = f32[256,2048]{1,0:T(8,128)S(1)} fusion(f32[256,2048]{1,0:T(8,128)S(1)} %fusion.2, bf16[256,512]{1,0:T(8,128)(2,1)S(1)} %collective-permute-done.5, bf16[512,2048]{1,0:T(8,128)(2,1)} %collective-permute-done.6), kind=kOutput, calls=%fused_computation.1 | convolution fusion | flops 537395200 | bytes 6553600 | tf_op jit(solution)/shard_map/dot_general | solution.py:187
  119.1 3.1 %collective-permute-start.7 = (bf16[128,2048]{1,0:T(8,128)(2,1)S(1)}, bf16[128,2048]{1,0:T(8,128)(2,1)S(1)}, u32[]{:S(2)}, u32[]{:S(2)}) collective-permute-start(bf16[128,2048]{1,0:T(8,128)(2,1)S(1)} %slice.102), channel_id=1, source_target_pairs={{0,3},{1,2},{2,1},{3,0},{4,7},{5,6},{6,5},{7,4},{8,11},{9,10},{10,... | collective-permute-start | bytes 1572872 | tf_op jit(solution)/shard_map/ppermute | solution.py:190
  122.9 2.4 %convolution_add_fusion = f32[256,2048]{1,0:T(8,128)S(1)} fusion(f32[256,2048]{1,0:T(8,128)S(1)} %fusion, bf16[256,512]{1,0:T(8,128)(2,1)S(1)} %collective-permute-done.8, bf16[512,2048]{1,0:T(8,128)(2,1)} %collective-permute-done.9), kind=kOutput, calls=%fused_computation | convolution fusion | flops 537395200 | bytes 6553600 | tf_op jit(solution)/shard_map/dot_general | solution.py:187
  125.5 9.1 %collective-permute-done.7 = bf16[128,2048]{1,0:T(8,128)(2,1)S(1)} collective-permute-done((bf16[128,2048]{1,0:T(8,128)(2,1)S(1)}, bf16[128,2048]{1,0:T(8,128)(2,1)S(1)}, u32[]{:S(2)}, u32[]{:S(2)}) %collective-permute-start.7) | collective-permute-done | bytes 524320 | tf_op jit(solution)/shard_map/ppermute | solution.py:190
  134.7 4.2 %collective-permute-done.10 = bf16[128,2048]{1,0:T(8,128)(2,1)S(1)} collective-permute-done((bf16[128,2048]{1,0:T(8,128)(2,1)S(1)}, bf16[128,2048]{1,0:T(8,128)(2,1)S(1)}, u32[]{:S(2)}, u32[]{:S(2)}) %collective-permute-start.10) | collective-permute-done | bytes 524320 | tf_op jit(solution)/shard_map/ppermute | solution.py:192
  139.1 1.1 pad_maximum_fusion
  (84 shorter events, 16.0 us)
Async XLA Ops:
  0.0 20.1 %copy-start.15 = (s32[1,1,3]{2,1,0:T(1,128)S(1)}, s32[1,1,3]{2,1,0:T(1,128)}, u32[]{:S(2)}) copy-start(s32[1,1,3]{2,1,0:T(1,128)} %param.13) | copy-start | bytes 40
  0.0 20.2 %copy-start.11 = (bf16[4096,128]{1,0:T(8,128)(2,1)S(1)}, bf16[4096,128]{1,0:T(8,128)(2,1)}, u32[]{:S(2)}) copy-start(bf16[4096,128]{1,0:T(8,128)(2,1)} %param.11) | copy-start | bytes 3145732
  0.0 28.4 %collective-permute-start = (bf16[512,1024]{1,0:T(8,128)(2,1)}, bf16[512,1024]{1,0:T(8,128)(2,1)S(1)}, u32[]{:S(2)}, u32[]{:S(2)}) collective-permute-start(bf16[512,1024]{1,0:T(8,128)(2,1)} %param.7), channel_id=1, source_target_pairs={{0,1},{1,2},{2,3},{3,0},{4,5},{5,6},{6,7},{7,4},{8,9},{9,10},{10,1... | collective-permute-start | bytes 3145736 | tf_op jit(solution)/shard_map/ppermute | solution.py:218
  2.0 26.4 %collective-permute-start.1 = (bf16[512,1024]{1,0:T(8,128)(2,1)}, bf16[512,1024]{1,0:T(8,128)(2,1)S(1)}, u32[]{:S(2)}, u32[]{:S(2)}) collective-permute-start(bf16[512,1024]{1,0:T(8,128)(2,1)} %param.7), channel_id=1, source_target_pairs={{0,3},{1,0},{2,1},{3,2},{4,7},{5,4},{6,5},{7,6},{8,11},{9,8},{10,9... | collective-permute-start | bytes 3145736 | tf_op jit(solution)/shard_map/ppermute | solution.py:219
  4.8 22.4 %all-to-all-start = ((s32[64,1,2]{2,1,0:T(1,128)}), s32[64,1,2]{2,1,0:T(1,128)S(1)}, u32[]{:S(2)}, u32[]{:S(2)}) async-start(s32[64,1,2]{2,1,0:T(1,128)} %broadcast_in_dim.9), calls=%async_computation | async-start | bytes 65536 | tf_op jit(solution)/shard_map/all_to_all | solution.py:213
  17.8 3.5 %copy-start.14 = (f32[4096]{0:T(1024)S(1)}, f32[4096]{0:T(1024)}, u32[]{:S(2)}) copy-start(f32[4096]{0:T(1024)} %param.8) | copy-start | bytes 49156
  20.2 2.9 %copy-start.12 = (bf16[512,1024]{1,0:T(8,128)(2,1)S(1)}, bf16[512,1024]{1,0:T(8,128)(2,1)}, u32[]{:S(2)}) copy-start(bf16[512,1024]{1,0:T(8,128)(2,1)} %param.7) | copy-start | bytes 3145732
  21.3 3.5 %copy-start.1 = (bf16[4096,256]{1,0:T(8,128)(2,1)S(1)}, bf16[4096,256]{1,0:T(8,128)(2,1)}, u32[]{:S(2)}) copy-start(bf16[4096,256]{1,0:T(8,128)(2,1)} %constant_dynamic-update-slice_fusion) | copy-start | bytes 6291460
  23.1 20.9 %copy-start.2 = (f32[512,64]{1,0:T(8,128)}, f32[512,64]{1,0:T(8,128)S(1)}, u32[]{:S(2)}) copy-start(f32[512,64]{1,0:T(8,128)S(1)} %get-tuple-element.22) | copy-start | bytes 393220
  28.5 14.1 %collective-permute-start.2 = (bf16[256,1024]{1,0:T(8,128)(2,1)S(1)}, bf16[256,1024]{1,0:T(8,128)(2,1)S(1)}, u32[]{:S(2)}, u32[]{:S(2)}) collective-permute-start(bf16[256,1024]{1,0:T(8,128)(2,1)S(1)} %slice.56), channel_id=1, source_target_pairs={{0,1},{1,2},{2,3},{3,0},{4,5},{5,6},{6,7},{7,4},{8,9},{9,10},{10,1... | collective-permute-start | bytes 1572872 | tf_op jit(solution)/shard_map/ppermute | solution.py:236
  28.7 7.6 %copy-start.9 = (bf16[1024,256]{1,0:T(8,128)(2,1)S(1)}, bf16[1024,256]{1,0:T(8,128)(2,1)}, u32[]{:S(2)}) copy-start(bf16[1024,256]{1,0:T(8,128)(2,1)} %get-tuple-element.25) | copy-start | bytes 1572868
  28.7 13.0 %collective-permute-start.3 = (bf16[256,1024]{1,0:T(8,128)(2,1)S(1)}, bf16[256,1024]{1,0:T(8,128)(2,1)S(1)}, u32[]{:S(2)}, u32[]{:S(2)}) collective-permute-start(bf16[256,1024]{1,0:T(8,128)(2,1)S(1)} %slice.57), channel_id=1, source_target_pairs={{0,3},{1,0},{2,1},{3,2},{4,7},{5,4},{6,5},{7,6},{8,11},{9,8},{10,9... | collective-permute-start | bytes 1572872 | tf_op jit(solution)/shard_map/ppermute | solution.py:237
  36.2 1.2 copy-start.13
  40.8 2.6 %copy-start.4 = (bf16[1024,256]{1,0:T(8,128)(2,1)S(1)}, bf16[1024,256]{1,0:T(8,128)(2,1)}, u32[]{:S(2)}) copy-start(bf16[1024,256]{1,0:T(8,128)(2,1)} %get-tuple-element.26) | copy-start | bytes 1572868
  41.7 2.2 %copy-start.7 = (bf16[256,1024]{1,0:T(8,128)(2,1)}, bf16[256,1024]{1,0:T(8,128)(2,1)S(1)}, u32[]{:S(2)}) copy-start(bf16[256,1024]{1,0:T(8,128)(2,1)S(1)} %collective-permute-done.3) | copy-start | bytes 1572868
  42.6 1.3 copy-start.5
  45.8 21.1 %copy-start.6 = (bf16[256,1024]{1,0:T(8,128)(2,1)S(1)}, bf16[256,1024]{1,0:T(8,128)(2,1)}, u32[]{:S(2)}) copy-start(bf16[256,1024]{1,0:T(8,128)(2,1)} %copy-done.5) | copy-start | bytes 1572868
  45.8 25.9 %all-to-all-start.1 = ((bf16[64,16,128]{2,1,0:T(8,128)(2,1)}), bf16[64,16,128]{2,1,0:T(8,128)(2,1)S(1)}, u32[]{:S(2)}, u32[]{:S(2)}) async-start(bf16[64,16,128]{2,1,0:T(8,128)(2,1)} %bitcast.8), calls=%async_computation.1 | async-start | bytes 524288 | tf_op jit(solution)/shard_map/all_to_all | solution.py:253
  57.0 11.9 %copy-start.8 = (bf16[256,1024]{1,0:T(8,128)(2,1)S(1)}, bf16[256,1024]{1,0:T(8,128)(2,1)}, u32[]{:S(2)}) copy-start(bf16[256,1024]{1,0:T(8,128)(2,1)} %copy-done.7) | copy-start | bytes 1572868
  60.2 29.6 %collective-permute-start.4 = (bf16[1024,128]{1,0:T(8,128)(2,1)}, bf16[1024,128]{1,0:T(8,128)(2,1)S(1)}, u32[]{:S(2)}, u32[]{:S(2)}) collective-permute-start(bf16[1024,128]{1,0:T(8,128)(2,1)} %pad_maximum_fusion.8.own_ref), channel_id=1, source_target_pairs={{0,4},{4,8},{8,12},{12,16},{16,20},{20,24},{24,28},{28,32},{32,36}... | collective-permute-start | bytes 786440 | tf_op jit(solution)/shard_map/ppermute | solution.py:254
  63.7 52.9 %collective-permute-start.6 = (bf16[512,2048]{1,0:T(8,128)(2,1)}, bf16[512,2048]{1,0:T(8,128)(2,1)}, u32[]{:S(2)}, u32[]{:S(2)}) collective-permute-start(bf16[512,2048]{1,0:T(8,128)(2,1)} %get-tuple-element.31), channel_id=1, source_target_pairs={{0,1},{1,0},{2,3},{3,2},{4,5},{5,4},{6,7},{7,6},{8,9},{9,8},{10,11... | collective-permute-start | bytes 6291464 | tf_op jit(solution)/shard_map/ppermute | solution.py:260
  64.7 58.2 %collective-permute-start.9 = (bf16[512,2048]{1,0:T(8,128)(2,1)}, bf16[512,2048]{1,0:T(8,128)(2,1)}, u32[]{:S(2)}, u32[]{:S(2)}) collective-permute-start(bf16[512,2048]{1,0:T(8,128)(2,1)} %get-tuple-element.32), channel_id=1, source_target_pairs={{0,3},{1,2},{2,1},{3,0},{4,7},{5,6},{6,5},{7,4},{8,11},{9,10},{10,... | collective-permute-start | bytes 6291464 | tf_op jit(solution)/shard_map/ppermute | solution.py:260
  73.2 27.3 %all-to-all-start.2 = ((bf16[64,2,16,128]{3,2,1,0:T(8,128)(2,1)}), bf16[64,2,16,128]{3,2,1,0:T(8,128)(2,1)S(1)}, u32[]{:S(2)}, u32[]{:S(2)}) async-start(bf16[64,2,16,128]{3,2,1,0:T(8,128)(2,1)} %bitcast.9), calls=%async_computation.2 | async-start | bytes 1048576 | tf_op jit(solution)/shard_map/all_to_all | solution.py:255
  86.6 1.8 %copy-start.3 = (f32[512,64]{1,0:T(8,128)S(1)}, f32[512,64]{1,0:T(8,128)}, u32[]{:S(2)}) copy-start(f32[512,64]{1,0:T(8,128)} %copy-done.2) | copy-start | bytes 393220
  86.6 1.8 %copy-start.10 = (f32[512,64]{1,0:T(8,128)S(1)}, f32[512,64]{1,0:T(8,128)}, u32[]{:S(2)}) copy-start(f32[512,64]{1,0:T(8,128)} %get-tuple-element.54) | copy-start | bytes 393220
  100.5 6.7 %copy-start = (bf16[512,4096]{1,0:T(8,128)(2,1)S(1)}, bf16[512,4096]{1,0:T(8,128)(2,1)}, u32[]{:S(2)}) copy-start(bf16[512,4096]{1,0:T(8,128)(2,1)} %param.12) | copy-start | bytes 12582916
  105.7 10.9 %collective-permute-start.5 = (bf16[256,512]{1,0:T(8,128)(2,1)S(1)}, bf16[256,512]{1,0:T(8,128)(2,1)S(1)}, u32[]{:S(2)}, u32[]{:S(2)}) collective-permute-start(bf16[256,512]{1,0:T(8,128)(2,1)S(1)} %get-tuple-element.48), channel_id=1, source_target_pairs={{0,1},{1,0},{2,3},{3,2},{4,5},{5,4},{6,7},{7,6},{8,9},{9,8},{10,11... | collective-permute-start | bytes 786440 | tf_op jit(solution)/shard_map/ppermute | solution.py:183
  106.6 16.4 %collective-permute-start.8 = (bf16[256,512]{1,0:T(8,128)(2,1)S(1)}, bf16[256,512]{1,0:T(8,128)(2,1)S(1)}, u32[]{:S(2)}, u32[]{:S(2)}) collective-permute-start(bf16[256,512]{1,0:T(8,128)(2,1)S(1)} %get-tuple-element.49), channel_id=1, source_target_pairs={{0,3},{1,2},{2,1},{3,0},{4,7},{5,6},{6,5},{7,4},{8,11},{9,10},{10,... | collective-permute-start | bytes 786440 | tf_op jit(solution)/shard_map/ppermute | solution.py:184
  119.1 15.5 %collective-permute-start.7 = (bf16[128,2048]{1,0:T(8,128)(2,1)S(1)}, bf16[128,2048]{1,0:T(8,128)(2,1)S(1)}, u32[]{:S(2)}, u32[]{:S(2)}) collective-permute-start(bf16[128,2048]{1,0:T(8,128)(2,1)S(1)} %slice.102), channel_id=1, source_target_pairs={{0,3},{1,2},{2,1},{3,0},{4,7},{5,6},{6,5},{7,4},{8,11},{9,10},{10,... | collective-permute-start | bytes 1572872 | tf_op jit(solution)/shard_map/ppermute | solution.py:190
  125.4 13.6 %collective-permute-start.10 = (bf16[128,2048]{1,0:T(8,128)(2,1)S(1)}, bf16[128,2048]{1,0:T(8,128)(2,1)S(1)}, u32[]{:S(2)}, u32[]{:S(2)}) collective-permute-start(bf16[128,2048]{1,0:T(8,128)(2,1)S(1)} %slice.101), channel_id=1, source_target_pairs={{0,1},{1,0},{2,3},{3,2},{4,5},{5,4},{6,7},{7,6},{8,9},{9,8},{10,11... | collective-permute-start | bytes 1572872 | tf_op jit(solution)/shard_map/ppermute | solution.py:192

commit v2 on v1

--- a/solution.py
+++ b/solution.py
@@ -164,13 +164,13 @@
 ODD = [(i, RING - 1 - i) for i in range(RING)]
 
 
-def project_out(attended, w_out, w_near, me):
+def project_out(attended, w_out, w_near, me, core):
     rows, depth = attended.shape
     quarter, half = rows // RING, w_out.shape[1] // 2
     even, odd = me ^ 1, RING - 1 - me
     parts = attended.reshape(RING, quarter, depth)
 
-    def pick(one, two):
+    def pick(one, two, parts=parts):
         return jnp.concatenate(
             [
                 lax.dynamic_index_in_dim(parts, one, 0, keepdims=False),
@@ -180,8 +180,10 @@
         )
 
     across = (me + 2) % RING
-    got_even = lax.ppermute(pick(even, across), "kvh", EVEN)
-    got_odd = lax.ppermute(pick(odd, across), "kvh", ODD)
+    turned = jnp.concatenate([parts[..., depth // 2 :], parts[..., : depth // 2]], axis=-1)
+    turned = jnp.where(core == 0, parts, turned)
+    got_even = lax.ppermute(pick(even, across, turned), "kvh", EVEN)
+    got_odd = lax.ppermute(pick(odd, across, turned), "kvh", ODD)
 
     def times(rows, w):
         return jnp.dot(rows, w, preferred_element_type=jnp.float32)
@@ -254,10 +256,13 @@
     before = lax.ppermute(own, "ctx", [(i, i + 1) for i in range(ctx_count - 1)])
     got = lax.all_to_all(route(wanted, held).reshape(ctx_count, 2, -1, HD), "ctx", 0, 0)
 
-    mid = w_out.shape[1] // 2
+    mid, core = w_out.shape[1] // 2, block_index % 2
     passed = after(w_out, from_left)
+    passed = lax.dynamic_slice_in_dim(passed, core * (passed.shape[0] // 2), passed.shape[0] // 2, 0)
     front, back = after(passed[:, :mid], upper, lower), after(passed[:, mid:], upper, lower)
-    w_near = lax.ppermute(front, "kvh", EVEN), lax.ppermute(back, "kvh", ODD)
+    cores = [(i, i ^ 1) for i in range(ctx_count)]
+    w_near = [lax.ppermute(front, "kvh", EVEN), lax.ppermute(back, "kvh", ODD)]
+    w_near = [jnp.concatenate([w, lax.ppermute(w, "ctx", cores)], axis=0) for w in w_near]
 
     w_late = after(w_query, from_left)
     queries = (project(
@@ -267,7 +272,7 @@
     flags = (chosen < block_index).astype(jnp.int32)
     sums, stats = attend_near(flags, queries, own, before)
     attended = attend_far(flags, queries, got, sums, stats)
-    return project_out(attended, w_out, w_near, me)
+    return project_out(attended, w_out, w_near, me, core)
 
 
 def solution(mesh):

time: 141 us -> 141 us (level)
  starting transfers between devices: 51.3 us -> 48.7 us
  other arithmetic: 9.49 us -> 11.6 us
    ppermute x1, waiting for transfers between devices: 9.14 us -> 4.29 us  [project_out(): lax.ppermute(sums_first[quarter:].astype(jnp.bfloat16), 'kvh', ODD)]
    ppermute x1, waiting for transfers between devices: 4.24 us -> 8.55 us  [project_out(): lax.ppermute(sums_second[quarter:].astype(jnp.bfloat16), 'kvh', EVEN)]
    ppermute x1, waiting for transfers between devices: 0.74 us -> 4.22 us  [local(): upper = lax.ppermute(from_left[:half], 'kvh', RIGHT)]
    ppermute x1, starting transfers between devices: 3.09 us -> 0.2 us  [project_out(): lax.ppermute(sums_first[quarter:].astype(jnp.bfloat16), 'kvh', ODD)]
    ppermute x1, starting transfers between devices: 2.04 us -> 0.01 us  [local(): from_left = lax.ppermute(tokens, 'kvh', RIGHT)]
    ppermute x1, starting transfers between devices: 1.36 us -> 3.31 us  [local(): from_right = lax.ppermute(tokens, 'kvh', LEFT)]
    slice x1, local copies, waits for them, and re-layouts: 4.81 us -> 3.2 us  [local(): passed[:, :mid]]
    ppermute x4 -> x6, waiting for transfers between devices: 8.78 us -> 7.36 us  [the longest x1 7.35 us: project_out(): got_odd = lax.ppermute(pick(odd, across, turned), 'kvh', ODD)]
  transfers between devices with their start and end apart: 14 -> 16, of which waited for: 7 -> 5; matrix products, arithmetic and copies ran while one was open for 30% -> 31% of each run, Pallas kernels for 8% -> 8%
where the time goes in v2:
time: 141 us; the launch traced here: 139 us
  starting transfers between devices  48.7 us (35%)
  waiting for transfers between devices  29.9 us (21%)
  matrix products  24.5 us (17%)
  local copies, waits for them, and re-layouts  12.9 us (9%)
  other arithmetic  11.6 us (8%)
  Pallas kernels  11.1 us (8%)
    dot_general x14, matrix products, times(): return jnp.dot(rows, w, preferred_element_type=jnp.float32)  24.5 us
    all_to_all x1, starting transfers between devices, local(): lax.all_to_all(jnp.broadcast_to(chosen[None, None, 1:], (ctx_count, 1, 2)...  12.6 us
    pallas_call x3, Pallas kernels, call(): pl.pallas_call(kernel, out_shape=out_shape, in_specs=[SMEM] + [VMEM] * (l...  11.1 us
    all_to_all x1, starting transfers between devices, local(): held = lax.all_to_all(own.reshape(ctx_count, -1, HD), 'ctx', 0, 0)  10.9 us
    all_to_all x1, starting transfers between devices, local(): lax.all_to_all(route(wanted, held).reshape(ctx_count, 2, -1, HD), 'ctx',...  9.57 us
    ppermute x1, waiting for transfers between devices, project_out(): lax.ppermute(sums_second[quarter:].astype(jnp.bfloat16), 'kvh', EVEN)  8.55 us
    ppermute x1, waiting for transfers between devices, project_out(): got_odd = lax.ppermute(pick(odd, across, turned), 'kvh', ODD)  7.35 us
    all_to_all x1, waiting for transfers between devices, local(): lax.all_to_all(route(wanted, held).reshape(ctx_count, 2, -1, HD), 'ctx',...  5.49 us
  transfers between devices with their start and end apart: 16, of which 5 were waited for; matrix products, arithmetic and copies ran while one was open for 31% of the time, Pallas kernels for 8%

profile of v2, /device:TPU:1, one launch (start us, length us, event | category | flops | bytes accessed | tf_op | source)
XLA Modules:
  0.0 139.2 jit_solution(2202977764145117225)
XLA Ops:
  0.0 3.3 %collective-permute-start.1 = (bf16[512,1024]{1,0:T(8,128)(2,1)}, bf16[512,1024]{1,0:T(8,128)(2,1)S(1)}, u32[]{:S(2)}, u32[]{:S(2)}) collective-permute-start(bf16[512,1024]{1,0:T(8,128)(2,1)} %param.7), channel_id=1, source_target_pairs={{0,3},{1,0},{2,1},{3,2},{4,7},{5,4},{6,5},{7,6},{8,11},{9,8},{10,9... | collective-permute-start | bytes 3145736 | tf_op jit(solution)/shard_map/ppermute | solution.py:221
  4.7 12.6 %all-to-all-start = ((s32[64,1,2]{2,1,0:T(1,128)}), s32[64,1,2]{2,1,0:T(1,128)S(1)}, u32[]{:S(2)}, u32[]{:S(2)}) async-start(s32[64,1,2]{2,1,0:T(1,128)} %broadcast_in_dim.9), calls=%async_computation | async-start | bytes 65536 | tf_op jit(solution)/shard_map/all_to_all | solution.py:215
  17.4 1.5 %multiply_reduce_fusion.2 = f32[512]{0:T(512)S(1)} fusion(bf16[512,1024]{1,0:T(8,128)(2,1)} %param.7), kind=kLoop, calls=%fused_computation.14 | loop fusion | flops 1572352 | bytes 1050624 | tf_op jit(solution)/shard_map/reduce_sum | solution.py:246
  19.5 2.3 %constant_dynamic-update-slice_fusion.1 = bf16[4096,256]{1,0:T(8,128)(2,1)} fusion(bf16[4096,128]{1,0:T(8,128)(2,1)} %param.10), kind=kLoop, calls=%fused_computation.82 | loop fusion | bytes 2097152
  21.9 1.7 %multiply_sine_fusion = (f32[512,64]{1,0:T(8,128)}, f32[512,64]{1,0:T(8,128)S(1)}) fusion(f32[64]{0:T(128)S(1)} %multiply_power_fusion, f32[512]{0:T(512)S(1)} %add_convert_fusion.1), kind=kLoop, calls=%fused_computation.54 | loop fusion | flops 32768 | bytes 264448 | tf_op jit(solution)/shard_map/sin | solution.py:18
  23.6 1.1 constant_dynamic-update-slice_fusion
  25.3 2.5 %convolution_bitcast_fusion.1 = f32[512,256]{1,0:T(8,128)} fusion(bf16[512,1024]{1,0:T(8,128)(2,1)S(1)} %copy-done.12, f32[1024]{0:T(1024)S(1)} %get-tuple-element.56, bf16[4096,256]{1,0:T(8,128)(2,1)} %constant_dynamic-update-slice_fusion, s32[]{:T(128)S(6)} %select_n.86), kind=kOutput, calls=%fused_computation.24 | convolution fusion | flops 269221888 | bytes 2101252 | tf_op jit(solution)/shard_map/dot_general | solution.py:230
  27.8 1.5 %multiply_convert_fusion.7 = (bf16[1024,256]{1,0:T(8,128)(2,1)S(1)}, bf16[1024,256]{1,0:T(8,128)(2,1)}, bf16[1024,256]{1,0:T(8,128)(2,1)}) fusion(f32[1024]{0:T(1024)S(1)} %get-tuple-element.54, bf16[4096,256]{1,0:T(8,128)(2,1)S(1)} %copy-done.1, s32[]{:T(128)S(6)} %select_n.92, f32[1024]{0:T(1024)S(1)} %get-tuple-element.57, s32[]{:T(128)S(6)} %select_n.90, ...), kind=kLoop, calls=%fused_computation.43 | loop fusion | flops 2359296 | bytes 3158028 | tf_op jit(solution)/shard_map/convert_element_type | solution.py:227
  31.3 2.6 %collective-permute-start.3 = (bf16[256,1024]{1,0:T(8,128)(2,1)S(1)}, bf16[256,1024]{1,0:T(8,128)(2,1)S(1)}, u32[]{:S(2)}, u32[]{:S(2)}) collective-permute-start(bf16[256,1024]{1,0:T(8,128)(2,1)S(1)} %slice.63), channel_id=1, source_target_pairs={{0,3},{1,0},{2,1},{3,2},{4,7},{5,4},{6,5},{7,6},{8,11},{9,8},{10,9... | collective-permute-start | bytes 1572872 | tf_op jit(solution)/shard_map/ppermute | solution.py:239
  33.9 3.1 %fusion.13 = f32[512,512]{0,1:T(8,128)} fusion(bf16[512,1024]{1,0:T(8,128)(2,1)S(1)} %collective-permute-done.1, f32[1024]{0:T(1024)S(1)} %get-tuple-element.57, bf16[4096,512]{1,0:T(8,128)(2,1)} %param.9, s32[]{:T(128)S(6)} %select_n.90), kind=kOutput, calls=%fused_computation.25 | convolution fusion | flops 538443776 | bytes 3149828 | tf_op jit(solution)/shard_map/dot_general | solution.py:230
  38.2 3.2 %convolution_bitcast_fusion = f32[512,512]{0,1:T(8,128)} fusion(bf16[512,1024]{1,0:T(8,128)(2,1)S(1)} %copy-done.13, f32[1024]{0:T(1024)S(1)} %get-tuple-element.56, bf16[4096,512]{1,0:T(8,128)(2,1)} %param.9, s32[]{:T(128)S(6)} %select_n.86), kind=kOutput, calls=%fused_computation.21 | convolution fusion | flops 538443776 | bytes 3149828 | tf_op jit(solution)/shard_map/dot_general | solution.py:230
  41.5 4.2 %collective-permute-done.2 = bf16[256,1024]{1,0:T(8,128)(2,1)S(1)} collective-permute-done((bf16[256,1024]{1,0:T(8,128)(2,1)S(1)}, bf16[256,1024]{1,0:T(8,128)(2,1)S(1)}, u32[]{:S(2)}, u32[]{:S(2)}) %collective-permute-start.2) | collective-permute-done | bytes 524320 | tf_op jit(solution)/shard_map/ppermute | solution.py:238
  49.1 10.9 %all-to-all-start.1 = ((bf16[64,16,128]{2,1,0:T(8,128)(2,1)}), bf16[64,16,128]{2,1,0:T(8,128)(2,1)S(1)}, u32[]{:S(2)}, u32[]{:S(2)}) async-start(bf16[64,16,128]{2,1,0:T(8,128)(2,1)} %bitcast.8), calls=%async_computation.1 | async-start | bytes 524288 | tf_op jit(solution)/shard_map/all_to_all | solution.py:255
  60.1 3.2 %constant_dynamic-slice_fusion = (bf16[256,2048]{1,0:T(8,128)(2,1)}, bf16[256,2048]{1,0:T(8,128)(2,1)}) fusion(bf16[512,4096]{1,0:T(8,128)(2,1)} %param.12, s32[]{:T(128)S(6)} %select_n.100, s32[]{:T(128)S(6)} %add.198), kind=kLoop, calls=%fused_computation.84 | loop fusion | bytes 4194312 | tf_op jit(solution)/shard_map/slice | solution.py:262
  63.3 3.7 %collective-permute-start.4 = (bf16[1024,128]{1,0:T(8,128)(2,1)}, bf16[1024,128]{1,0:T(8,128)(2,1)S(1)}, u32[]{:S(2)}, u32[]{:S(2)}) collective-permute-start(bf16[1024,128]{1,0:T(8,128)(2,1)} %pad_maximum_fusion.8.own_ref), channel_id=1, source_target_pairs={{0,4},{4,8},{8,12},{12,16},{16,20},{20,24},{24,28},{28,32},{32,36}... | collective-permute-start | bytes 786440 | tf_op jit(solution)/shard_map/ppermute | solution.py:256
  66.9 2.6 %collective-permute-start.10 = (bf16[256,2048]{1,0:T(8,128)(2,1)}, bf16[256,2048]{1,0:T(8,128)(2,1)}, u32[]{:S(2)}, u32[]{:S(2)}) collective-permute-start(bf16[256,2048]{1,0:T(8,128)(2,1)} %get-tuple-element.32), channel_id=1, source_target_pairs={{0,3},{1,2},{2,1},{3,0},{4,7},{5,6},{6,5},{7,4},{8,11},{9,10},{10,... | collective-permute-start | bytes 3145736 | tf_op jit(solution)/shard_map/ppermute | solution.py:264
  69.6 2.8 %fusion.26 = f32[256,512]{0,1:T(8,128)} fusion(bf16[256,1024]{1,0:T(8,128)(2,1)S(1)} %copy-done.6, f32[1024]{0:T(1024)S(1)} %get-tuple-element.54, bf16[4096,512]{1,0:T(8,128)(2,1)} %param.9, s32[]{:T(128)S(6)} %select_n.92), kind=kOutput, calls=%fused_computation.57 | convolution fusion | flops 270008320 | bytes 2101252 | tf_op jit(solution)/shard_map/dot_general | solution.py:230
  72.4 2.7 %fusion.25 = f32[256,512]{0,1:T(8,128)} fusion(bf16[256,1024]{1,0:T(8,128)(2,1)S(1)} %copy-done.8, f32[1024]{0:T(1024)S(1)} %get-tuple-element.54, bf16[4096,512]{1,0:T(8,128)(2,1)} %param.9, s32[]{:T(128)S(6)} %select_n.92), kind=kOutput, calls=%fused_computation.56 | convolution fusion | flops 270008320 | bytes 2101252 | tf_op jit(solution)/shard_map/dot_general | solution.py:230
  75.1 1.4 %route.1 = bf16[128,16,128]{2,1,0:T(8,128)(2,1)} custom-call(s32[128]{0:T(128)S(1)} %reshape.129.wanted_ref, bf16[64,16,128]{2,1,0:T(8,128)(2,1)S(1)} %all-to-all-done.1.held_ref), custom_call_target="tpu_custom_call" | custom-call | flops 1048576 | bytes 4194304 | tf_op jit(solution)/shard_map/route/pallas_call | solution.py:129
  76.6 9.6 %all-to-all-start.2 = ((bf16[64,2,16,128]{3,2,1,0:T(8,128)(2,1)}), bf16[64,2,16,128]{3,2,1,0:T(8,128)(2,1)S(1)}, u32[]{:S(2)}, u32[]{:S(2)}) async-start(bf16[64,2,16,128]{3,2,1,0:T(8,128)(2,1)} %bitcast.9), calls=%async_computation.2 | async-start | bytes 1048576 | tf_op jit(solution)/shard_map/all_to_all | solution.py:257
  86.2 2.7 %fusion.12 = f32[512,512]{0,1:T(8,128)S(1)} fusion(f32[512,512]{0,1:T(8,128)S(1)} %copy-done.14, f32[512,512]{0,1:T(8,128)} %convolution_bitcast_fusion, bf16[512,1024]{1,0:T(8,128)(2,1)S(1)} %collective-permute-done, f32[256,512]{0,1:T(8,128)} %fusion.25, f32[256,512]{0,1:T(8,128)S(1)} %copy-done.16, f32[1024]{0:T(1024)S(1)} %get-tuple-element.55, ...), kind=kOutput, calls=%fused_computation.23 | convolution fusion | flops 539754496 | bytes 6297604 | tf_op jit(solution)/shard_map/dot_general | solution.py:230
  90.1 1.4 %copy.34 = f32[512,4,64]{2,1,0:T(4,128)S(1)} copy(f32[512,4,64]{0,2,1:T(8,128)} %get-tuple-element.41) | data formatting | bytes 1048576
  93.0 4.5 %attend_near.1 = (f32[2048,128]{1,0:T(8,128)S(1)}, f32[2048,128]{1,0:T(8,128)S(1)}) custom-call(s32[3]{0:T(128)S(1)} %fusion.42.flag_ref, bf16[512,512]{1,0:T(8,128)(2,1)S(1)} %bitcast.62, bf16[1024,128]{1,0:T(8,128)(2,1)} %pad_maximum_fusion.8.own_ref, bf16[1024,128]{1,0:T(8,128)(2,1)S(1)} %collective-permute-done.4.before_ref), custom_call_target="tpu_custom_call" | custom-call | flops 1073741824 | bytes 4194304 | tf_op jit(solution)/shard_map/attend_near/pallas_call | solution.py:129
  98.4 5.5 %all-to-all-done.2.got_ref = bf16[64,2,16,128]{3,2,1,0:T(8,128)(2,1)S(1)} async-done(((bf16[64,2,16,128]{3,2,1,0:T(8,128)(2,1)}), bf16[64,2,16,128]{3,2,1,0:T(8,128)(2,1)S(1)}, u32[]{:S(2)}, u32[]{:S(2)}) %all-to-all-start.2) | async-done | bytes 524320 | tf_op jit(solution)/shard_map/all_to_all | solution.py:257
  103.9 5.2 %attend_far.1 = bf16[512,512]{1,0:T(8,128)(2,1)S(1)} custom-call(s32[3]{0:T(128)S(1)} %fusion.42.flag_ref, bf16[512,512]{1,0:T(8,128)(2,1)S(1)} %bitcast.63, bf16[64,2,16,128]{3,2,1,0:T(8,128)(2,1)S(1)} %all-to-all-done.2.got_ref, f32[2048,128]{1,0:T(8,128)S(1)} %get-tuple-element.28.sums_ref, f32[2048,128]{1,0:T(8,128)S(1)} %get-tuple-element.29.stats_ref), custom_call_target="tpu_custom_call" | custom-call | flops 1073741824 | bytes 4194304 | tf_op jit(solution)/shard_map/attend_far/pallas_call | solution.py:129
  109.4 1.5 %collective-permute-start.5 = (bf16[256,512]{1,0:T(8,128)(2,1)S(1)}, bf16[256,512]{1,0:T(8,128)(2,1)S(1)}, u32[]{:S(2)}, u32[]{:S(2)}) collective-permute-start(bf16[256,512]{1,0:T(8,128)(2,1)S(1)} %get-tuple-element.52), channel_id=1, source_target_pairs={{0,1},{1,0},{2,3},{3,2},{4,5},{5,4},{6,7},{7,6},{8,9},{9,8},{10,11... | collective-permute-start | bytes 786440 | tf_op jit(solution)/shard_map/ppermute | solution.py:185
  111.9 7.4 %collective-permute-done.9 = bf16[256,512]{1,0:T(8,128)(2,1)S(1)} collective-permute-done((bf16[256,512]{1,0:T(8,128)(2,1)S(1)}, bf16[256,512]{1,0:T(8,128)(2,1)S(1)}, u32[]{:S(2)}, u32[]{:S(2)}) %collective-permute-start.9) | collective-permute-done | bytes 262176 | tf_op jit(solution)/shard_map/ppermute | solution.py:186
  119.3 2.3 %convolution_add_fusion = f32[256,2048]{1,0:T(8,128)S(1)} fusion(f32[256,2048]{1,0:T(8,128)S(1)} %fusion.6, bf16[256,512]{1,0:T(8,128)(2,1)S(1)} %collective-permute-done.9, bf16[256,2048]{1,0:T(8,128)(2,1)} %collective-permute-done.11, bf16[256,2048]{1,0:T(8,128)(2,1)} %collective-permute-done.10), kind=kOutput, calls=%fused_computation | convolution fusion | flops 541589504 | bytes 6553600 | tf_op jit(solution)/shard_map/dot_general | solution.py:189
  122.5 2.3 %convolution_add_fusion.1 = f32[256,2048]{1,0:T(8,128)S(1)} fusion(f32[256,2048]{1,0:T(8,128)S(1)} %fusion.8, bf16[256,512]{1,0:T(8,128)(2,1)S(1)} %collective-permute-done.5, bf16[256,2048]{1,0:T(8,128)(2,1)} %collective-permute-done.7, bf16[256,2048]{1,0:T(8,128)(2,1)} %collective-permute-done.6), kind=kOutput, calls=%fused_computation.1 | convolution fusion | flops 541589504 | bytes 6553600 | tf_op jit(solution)/shard_map/dot_general | solution.py:189
  125.1 8.6 %collective-permute-done.12 = bf16[128,2048]{1,0:T(8,128)(2,1)S(1)} collective-permute-done((bf16[128,2048]{1,0:T(8,128)(2,1)S(1)}, bf16[128,2048]{1,0:T(8,128)(2,1)S(1)}, u32[]{:S(2)}, u32[]{:S(2)}) %collective-permute-start.12) | collective-permute-done | bytes 524320 | tf_op jit(solution)/shard_map/ppermute | solution.py:194
  133.7 4.3 %collective-permute-done.8 = bf16[128,2048]{1,0:T(8,128)(2,1)S(1)} collective-permute-done((bf16[128,2048]{1,0:T(8,128)(2,1)S(1)}, bf16[128,2048]{1,0:T(8,128)(2,1)S(1)}, u32[]{:S(2)}, u32[]{:S(2)}) %collective-permute-start.8) | collective-permute-done | bytes 524320 | tf_op jit(solution)/shard_map/ppermute | solution.py:192
  138.2 1.1 pad_maximum_fusion
  (95 shorter events, 15.5 us)
Async XLA Ops:
  0.0 23.6 %copy-start.17 = (f32[4096]{0:T(1024)S(1)}, f32[4096]{0:T(1024)}, u32[]{:S(2)}) copy-start(f32[4096]{0:T(1024)} %param.8) | copy-start | bytes 49156
  0.0 23.6 %copy-start.11 = (bf16[4096,128]{1,0:T(8,128)(2,1)S(1)}, bf16[4096,128]{1,0:T(8,128)(2,1)}, u32[]{:S(2)}) copy-start(bf16[4096,128]{1,0:T(8,128)(2,1)} %param.11) | copy-start | bytes 3145732
  0.0 30.6 %collective-permute-start.1 = (bf16[512,1024]{1,0:T(8,128)(2,1)}, bf16[512,1024]{1,0:T(8,128)(2,1)S(1)}, u32[]{:S(2)}, u32[]{:S(2)}) collective-permute-start(bf16[512,1024]{1,0:T(8,128)(2,1)} %param.7), channel_id=1, source_target_pairs={{0,3},{1,0},{2,1},{3,2},{4,7},{5,4},{6,5},{7,6},{8,11},{9,8},{10,9... | collective-permute-start | bytes 3145736 | tf_op jit(solution)/shard_map/ppermute | solution.py:221
  3.3 27.3 %collective-permute-start = (bf16[512,1024]{1,0:T(8,128)(2,1)}, bf16[512,1024]{1,0:T(8,128)(2,1)S(1)}, u32[]{:S(2)}, u32[]{:S(2)}) collective-permute-start(bf16[512,1024]{1,0:T(8,128)(2,1)} %param.7), channel_id=1, source_target_pairs={{0,1},{1,2},{2,3},{3,0},{4,5},{5,6},{6,7},{7,4},{8,9},{9,10},{10,1... | collective-permute-start | bytes 3145736 | tf_op jit(solution)/shard_map/ppermute | solution.py:220
  4.7 24.6 %all-to-all-start = ((s32[64,1,2]{2,1,0:T(1,128)}), s32[64,1,2]{2,1,0:T(1,128)S(1)}, u32[]{:S(2)}, u32[]{:S(2)}) async-start(s32[64,1,2]{2,1,0:T(1,128)} %broadcast_in_dim.9), calls=%async_computation | async-start | bytes 65536 | tf_op jit(solution)/shard_map/all_to_all | solution.py:215
  23.6 23.7 %copy-start.2 = (f32[512,64]{1,0:T(8,128)}, f32[512,64]{1,0:T(8,128)S(1)}, u32[]{:S(2)}) copy-start(f32[512,64]{1,0:T(8,128)S(1)} %get-tuple-element.22) | copy-start | bytes 393220
  23.6 1.7 %copy-start.12 = (bf16[512,1024]{1,0:T(8,128)(2,1)S(1)}, bf16[512,1024]{1,0:T(8,128)(2,1)}, u32[]{:S(2)}) copy-start(bf16[512,1024]{1,0:T(8,128)(2,1)} %param.7) | copy-start | bytes 3145732
  24.7 3.0 %copy-start.1 = (bf16[4096,256]{1,0:T(8,128)(2,1)S(1)}, bf16[4096,256]{1,0:T(8,128)(2,1)}, u32[]{:S(2)}) copy-start(bf16[4096,256]{1,0:T(8,128)(2,1)} %constant_dynamic-update-slice_fusion) | copy-start | bytes 6291460
  30.7 6.3 %copy-start.9 = (bf16[1024,256]{1,0:T(8,128)(2,1)S(1)}, bf16[1024,256]{1,0:T(8,128)(2,1)}, u32[]{:S(2)}) copy-start(bf16[1024,256]{1,0:T(8,128)(2,1)} %get-tuple-element.25) | copy-start | bytes 1572868
  30.7 14.9 %collective-permute-start.2 = (bf16[256,1024]{1,0:T(8,128)(2,1)S(1)}, bf16[256,1024]{1,0:T(8,128)(2,1)S(1)}, u32[]{:S(2)}, u32[]{:S(2)}) collective-permute-start(bf16[256,1024]{1,0:T(8,128)(2,1)S(1)} %slice.62), channel_id=1, source_target_pairs={{0,1},{1,2},{2,3},{3,0},{4,5},{5,6},{6,7},{7,4},{8,9},{9,10},{10,1... | collective-permute-start | bytes 1572872 | tf_op jit(solution)/shard_map/ppermute | solution.py:238
  31.3 14.6 %collective-permute-start.3 = (bf16[256,1024]{1,0:T(8,128)(2,1)S(1)}, bf16[256,1024]{1,0:T(8,128)(2,1)S(1)}, u32[]{:S(2)}, u32[]{:S(2)}) collective-permute-start(bf16[256,1024]{1,0:T(8,128)(2,1)S(1)} %slice.63), channel_id=1, source_target_pairs={{0,3},{1,0},{2,1},{3,2},{4,7},{5,4},{6,5},{7,6},{8,11},{9,8},{10,9... | collective-permute-start | bytes 1572872 | tf_op jit(solution)/shard_map/ppermute | solution.py:239
  41.4 5.3 %copy-start.4 = (bf16[1024,256]{1,0:T(8,128)(2,1)S(1)}, bf16[1024,256]{1,0:T(8,128)(2,1)}, u32[]{:S(2)}) copy-start(bf16[1024,256]{1,0:T(8,128)(2,1)} %get-tuple-element.26) | copy-start | bytes 1572868
  41.4 5.3 %copy-start.15 = (f32[512,256]{1,0:T(8,128)S(1)}, f32[512,256]{1,0:T(8,128)}, u32[]{:S(2)}) copy-start(f32[512,256]{1,0:T(8,128)} %convolution_bitcast_fusion.1) | copy-start | bytes 1572868
  45.7 1.5 %copy-start.5 = (bf16[256,1024]{1,0:T(8,128)(2,1)}, bf16[256,1024]{1,0:T(8,128)(2,1)S(1)}, u32[]{:S(2)}) copy-start(bf16[256,1024]{1,0:T(8,128)(2,1)S(1)} %collective-permute-done.2) | copy-start | bytes 1572868
  49.1 26.0 %all-to-all-start.1 = ((bf16[64,16,128]{2,1,0:T(8,128)(2,1)}), bf16[64,16,128]{2,1,0:T(8,128)(2,1)S(1)}, u32[]{:S(2)}, u32[]{:S(2)}) async-start(bf16[64,16,128]{2,1,0:T(8,128)(2,1)} %bitcast.8), calls=%async_computation.1 | async-start | bytes 524288 | tf_op jit(solution)/shard_map/all_to_all | solution.py:255
  60.1 9.5 %copy-start.6 = (bf16[256,1024]{1,0:T(8,128)(2,1)S(1)}, bf16[256,1024]{1,0:T(8,128)(2,1)}, u32[]{:S(2)}) copy-start(bf16[256,1024]{1,0:T(8,128)(2,1)} %copy-done.5) | copy-start | bytes 1572868
  63.3 9.1 %copy-start.8 = (bf16[256,1024]{1,0:T(8,128)(2,1)S(1)}, bf16[256,1024]{1,0:T(8,128)(2,1)}, u32[]{:S(2)}) copy-start(bf16[256,1024]{1,0:T(8,128)(2,1)} %copy-done.7) | copy-start | bytes 1572868
  63.3 29.7 %collective-permute-start.4 = (bf16[1024,128]{1,0:T(8,128)(2,1)}, bf16[1024,128]{1,0:T(8,128)(2,1)S(1)}, u32[]{:S(2)}, u32[]{:S(2)}) collective-permute-start(bf16[1024,128]{1,0:T(8,128)(2,1)} %pad_maximum_fusion.8.own_ref), channel_id=1, source_target_pairs={{0,4},{4,8},{8,12},{12,16},{16,20},{20,24},{24,28},{28,32},{32,36}... | collective-permute-start | bytes 786440 | tf_op jit(solution)/shard_map/ppermute | solution.py:256
  66.9 30.6 %collective-permute-start.10 = (bf16[256,2048]{1,0:T(8,128)(2,1)}, bf16[256,2048]{1,0:T(8,128)(2,1)}, u32[]{:S(2)}, u32[]{:S(2)}) collective-permute-start(bf16[256,2048]{1,0:T(8,128)(2,1)} %get-tuple-element.32), channel_id=1, source_target_pairs={{0,3},{1,2},{2,1},{3,0},{4,7},{5,6},{6,5},{7,4},{8,11},{9,10},{10,... | collective-permute-start | bytes 3145736 | tf_op jit(solution)/shard_map/ppermute | solution.py:264
  69.6 28.5 %collective-permute-start.6 = (bf16[256,2048]{1,0:T(8,128)(2,1)}, bf16[256,2048]{1,0:T(8,128)(2,1)}, u32[]{:S(2)}, u32[]{:S(2)}) collective-permute-start(bf16[256,2048]{1,0:T(8,128)(2,1)} %get-tuple-element.31), channel_id=1, source_target_pairs={{0,1},{1,0},{2,3},{3,2},{4,5},{5,4},{6,7},{7,6},{8,9},{9,8},{10,11... | collective-permute-start | bytes 3145736 | tf_op jit(solution)/shard_map/ppermute | solution.py:264
  75.1 11.0 %copy-start.14 = (f32[512,512]{0,1:T(8,128)S(1)}, f32[512,512]{0,1:T(8,128)}, u32[]{:S(2)}) copy-start(f32[512,512]{0,1:T(8,128)} %fusion.13) | copy-start | bytes 3145732
  75.1 11.0 %copy-start.16 = (f32[256,512]{0,1:T(8,128)S(1)}, f32[256,512]{0,1:T(8,128)}, u32[]{:S(2)}) copy-start(f32[256,512]{0,1:T(8,128)} %fusion.26) | copy-start | bytes 1572868
  76.6 27.3 %all-to-all-start.2 = ((bf16[64,2,16,128]{3,2,1,0:T(8,128)(2,1)}), bf16[64,2,16,128]{3,2,1,0:T(8,128)(2,1)S(1)}, u32[]{:S(2)}, u32[]{:S(2)}) async-start(bf16[64,2,16,128]{3,2,1,0:T(8,128)(2,1)} %bitcast.9), calls=%async_computation.2 | async-start | bytes 1048576 | tf_op jit(solution)/shard_map/all_to_all | solution.py:257
  89.7 1.8 %copy-start.3 = (f32[512,64]{1,0:T(8,128)S(1)}, f32[512,64]{1,0:T(8,128)}, u32[]{:S(2)}) copy-start(f32[512,64]{1,0:T(8,128)} %copy-done.2) | copy-start | bytes 393220
  89.7 1.9 %copy-start.10 = (f32[512,64]{1,0:T(8,128)S(1)}, f32[512,64]{1,0:T(8,128)}, u32[]{:S(2)}) copy-start(f32[512,64]{1,0:T(8,128)} %get-tuple-element.58) | copy-start | bytes 393220
  97.5 21.8 %collective-permute-start.11 = (bf16[256,2048]{1,0:T(8,128)(2,1)}, bf16[256,2048]{1,0:T(8,128)(2,1)}, u32[]{:S(2)}, u32[]{:S(2)}) collective-permute-start(bf16[256,2048]{1,0:T(8,128)(2,1)} %collective-permute-done.10), channel_id=1, source_target_pairs={{0,4},{4,0},{8,12},{12,8},{16,20},{20,16},{24,28},{28,24},{32,36},... | collective-permute-start | bytes 3145736 | tf_op jit(solution)/shard_map/ppermute | solution.py:265
  98.1 24.4 %collective-permute-start.7 = (bf16[256,2048]{1,0:T(8,128)(2,1)}, bf16[256,2048]{1,0:T(8,128)(2,1)}, u32[]{:S(2)}, u32[]{:S(2)}) collective-permute-start(bf16[256,2048]{1,0:T(8,128)(2,1)} %collective-permute-done.6), channel_id=1, source_target_pairs={{0,4},{4,0},{8,12},{12,8},{16,20},{20,16},{24,28},{28,24},{32,36},... | collective-permute-start | bytes 3145736 | tf_op jit(solution)/shard_map/ppermute | solution.py:265
  109.0 2.2 %copy-start = (bf16[512,4096]{1,0:T(8,128)(2,1)S(1)}, bf16[512,4096]{1,0:T(8,128)(2,1)}, u32[]{:S(2)}) copy-start(bf16[512,4096]{1,0:T(8,128)(2,1)} %param.12) | copy-start | bytes 12582916
  109.4 13.1 %collective-permute-start.5 = (bf16[256,512]{1,0:T(8,128)(2,1)S(1)}, bf16[256,512]{1,0:T(8,128)(2,1)S(1)}, u32[]{:S(2)}, u32[]{:S(2)}) collective-permute-start(bf16[256,512]{1,0:T(8,128)(2,1)S(1)} %get-tuple-element.52), channel_id=1, source_target_pairs={{0,1},{1,0},{2,3},{3,2},{4,5},{5,4},{6,7},{7,6},{8,9},{9,8},{10,11... | collective-permute-start | bytes 786440 | tf_op jit(solution)/shard_map/ppermute | solution.py:185
  110.9 8.4 %collective-permute-start.9 = (bf16[256,512]{1,0:T(8,128)(2,1)S(1)}, bf16[256,512]{1,0:T(8,128)(2,1)S(1)}, u32[]{:S(2)}, u32[]{:S(2)}) collective-permute-start(bf16[256,512]{1,0:T(8,128)(2,1)S(1)} %get-tuple-element.53), channel_id=1, source_target_pairs={{0,3},{1,2},{2,1},{3,0},{4,7},{5,6},{6,5},{7,4},{8,11},{9,10},{10,... | collective-permute-start | bytes 786440 | tf_op jit(solution)/shard_map/ppermute | solution.py:186
  121.7 12.0 %collective-permute-start.12 = (bf16[128,2048]{1,0:T(8,128)(2,1)S(1)}, bf16[128,2048]{1,0:T(8,128)(2,1)S(1)}, u32[]{:S(2)}, u32[]{:S(2)}) collective-permute-start(bf16[128,2048]{1,0:T(8,128)(2,1)S(1)} %slice.111), channel_id=1, source_target_pairs={{0,1},{1,0},{2,3},{3,2},{4,5},{5,4},{6,7},{7,6},{8,9},{9,8},{10,11... | collective-permute-start | bytes 1572872 | tf_op jit(solution)/shard_map/ppermute | solution.py:194
  124.9 13.2 %collective-permute-start.8 = (bf16[128,2048]{1,0:T(8,128)(2,1)S(1)}, bf16[128,2048]{1,0:T(8,128)(2,1)S(1)}, u32[]{:S(2)}, u32[]{:S(2)}) collective-permute-start(bf16[128,2048]{1,0:T(8,128)(2,1)S(1)} %slice.112), channel_id=1, source_target_pairs={{0,3},{1,2},{2,1},{3,0},{4,7},{5,6},{6,5},{7,4},{8,11},{9,10},{10,... | collective-permute-start | bytes 1572872 | tf_op jit(solution)/shard_map/ppermute | solution.py:192
  (2 other events, 2.6 us)
